TPU v7x, 256 devices: a whole 4x4x8 slice. The times are simulated.
256 devices in a mesh: dp: 32 (over x_hi, z, core), mp: 8 (over x_lo, y).
Axes of the slice: x: 4 (x_hi: 2, x_lo: 2; x = x_hi * 2 + x_lo), y: 4, z: 8, core: 2. Of those that a mesh axis runs over, the one named last changes fastest.
Arguments:
- image_emb: bfloat16 [16384, 1152], P(('dp', 'mp')), may hold values from -0.1796875 to 0.1796875
- text_emb: bfloat16 [16384, 1152], P(('dp', 'mp')), may hold values from -0.1796875 to 0.1796875
- log_temp: float32 [1], replicated, may hold values from 1.6 to 2.7
- bias: float32 [1], replicated, may hold values from -3 to -1
Outputs:
- image_grad: float32 [16384, 1152], P(('dp', 'mp'))
- text_grad: float32 [16384, 1152], P(('dp', 'mp'))
All inputs are finite; a program needn't handle non-finite values.
Results may differ from a plain program's by a relative error of at most 0.0057.
Values may be sent and summed in bfloat16 or wider, within the bound.
A program may use at most 64 MiB of HBM per device.

v0:
```python
import jax
import jax.numpy as jnp
from jax import lax
from jax.sharding import PartitionSpec as P

eps = 1e-06


def from_behind(block, axis, distance):
    devices = range(lax.axis_size(axis))
    route = [((i - distance) % len(devices), i) for i in devices]
    return lax.ppermute(block, axis, route)


def normalize(emb):
    wide = emb.astype(jnp.float32)
    inverse = lax.rsqrt(jnp.sum(wide * wide, axis=1, keepdims=True) + eps)
    return (wide * inverse, inverse)


def back_norm(unit, inverse, grad):
    return inverse * (grad - unit * jnp.sum(unit * grad, axis=1, keepdims=True))


def pass_text(block):
    return from_behind(block, "dp", 1)


def pass_partial(partial_value):
    return from_behind(partial_value, "dp", 1)


def coef_of(q_rows, p_rows, txt_index, img_index, tau, shift_b):
    scores = lax.dot_general(
        q_rows, p_rows, (((1,), (1,)), ((), ())), preferred_element_type=jnp.float32
    )
    logits = tau * scores + shift_b
    label = jnp.where(txt_index[:, None] == img_index[None, :], jnp.float32(1.0), jnp.float32(-1.0))
    return (-tau * label * jax.nn.sigmoid(-label * logits)).astype(jnp.bfloat16)


def on_device(image_emb, text_emb, log_temp, bias):
    tau = jnp.exp(log_temp[0])
    shift_b = bias[0]
    rows = image_emb.shape[0]
    width = image_emb.shape[1]
    n_dp = lax.axis_size("dp")
    n_mp = lax.axis_size("mp")
    dp_pos = lax.axis_index("dp")
    mp_pos = lax.axis_index("mp")
    group = rows * n_mp
    unit_img, inv_img = normalize(image_emb)
    unit_txt, inv_txt = normalize(text_emb)
    p_own = unit_img.astype(jnp.bfloat16)
    q_own = unit_txt.astype(jnp.bfloat16)
    p_all = lax.all_gather(p_own, "mp", axis=0, tiled=True)
    img_index = dp_pos * group + jnp.arange(group, dtype=jnp.int32)
    row_range = jnp.arange(rows, dtype=jnp.int32)

    def block_coef(q_blk, owner):
        txt_index = owner * group + mp_pos * rows + row_range
        return coef_of(q_blk, p_all, txt_index, img_index, tau, shift_b)

    def block_terms(q_blk, owner):
        coef = block_coef(q_blk, owner)
        grad_q = jnp.dot(coef, p_all, preferred_element_type=jnp.float32)
        grad_p = lax.dot_general(
            coef, q_blk, (((0,), (0,)), ((), ())), preferred_element_type=jnp.float32
        )
        return (grad_q, grad_p)

    grad_p0 = jnp.zeros((group, width), jnp.float32)

    def carry_step(k, state):
        q_blk, partial_value, grad_p = state
        owner = (dp_pos - k) % n_dp
        grad_q, term = block_terms(q_blk, owner)
        partial_value = pass_partial(partial_value + grad_q)
        return (pass_text(q_blk), partial_value, grad_p + term)

    partial0 = jnp.zeros((rows, width), jnp.float32)
    q_blk, partial_value, grad_p = lax.fori_loop(
        0, n_dp - 1, carry_step, (q_own, partial0, grad_p0)
    )
    owner = (dp_pos - (n_dp - 1)) % n_dp
    grad_q, term = block_terms(q_blk, owner)
    grad_p = grad_p + term
    text_part = pass_partial(partial_value + grad_q)
    image_part = lax.psum_scatter(grad_p, "mp", scatter_dimension=0, tiled=True)
    return (back_norm(unit_img, inv_img, image_part), back_norm(unit_txt, inv_txt, text_part))


def solution(mesh):
    placed = (P(("dp", "mp"), None), P(("dp", "mp"), None), P(), P())
    return jax.shard_map(
        on_device,
        mesh=mesh,
        in_specs=placed,
        out_specs=(P(("dp", "mp"), None), P(("dp", "mp"), None)),
        check_vma=False,
    )
```

profile of v0, /device:TPU:1, one launch (start us, length us, event | category | flops | bytes accessed | tf_op | source)
XLA Modules:
  0.0 634.6 jit_solution(16877123209588532664)
XLA Ops:
  14.7 36.5 %all-gather.2.cloned.1.call-done = bf16[512,1152]{1,0:T(8,128)(2,1)} async-done(((bf16[64,1152]{1,0:T(8,128)(2,1)}), bf16[512,1152]{1,0:T(8,128)(2,1)}) %all-gather.2.cloned.1.call-update) | async-done | bytes 1179664 | tf_op jit(solution)/shard_map/all_gather | solution.py:56
  51.9 522.3 %while.20 = (s32[]{:T(128)}, bf16[64,1152]{1,0:T(8,128)(2,1)}, f32[64,1152]{1,0:T(8,128)}, f32[512,1152]{1,0:T(8,128)S(1)}, f32[]{:T(128)}, /*index=5*/s32[]{:T(...) while((s32[]{:T(128)}, bf16[64,1152]{1,0:T(8,128)(2,1)}, ...), condition=%wide.region_3.4_spmd.clone, body=%wide.region_2.3_spmd.clone.sunk | while | flops 228139600 | bytes 16389096 | solution.py:82
  53.6 6.6 %collective-permute-start = (bf16[64,1152]{1,0:T(8,128)(2,1)}, bf16[64,1152]{1,0:T(8,128)(2,1)}, u32[]{:S(2)}, u32[]{:S(2)}) collective-permute-start(bf16[64,1152]{1,0:T(8,128)(2,1)} %copy.11), channel_id=1, source_target_pairs={{248,0},{0,8},{8,16},{16,24},{24,32},{32,40},{40,48},{48,56},{56,6... | collective-permute-start | bytes 442376 | tf_op jit(solution)/shard_map/while/body/eval_jaxpr/ppermute | solution.py:12
  94.2 4.7 collective-permute-done.1
  128.1 4.7 collective-permute-done.1
  145.0 4.7 collective-permute-done.1
  178.9 4.7 collective-permute-done.1
  195.9 4.7 collective-permute-done.1
  229.8 4.7 collective-permute-done.1
  246.7 4.7 collective-permute-done.1
  280.7 4.7 collective-permute-done.1
  297.6 4.7 collective-permute-done.1
  331.5 4.7 collective-permute-done.1
  348.5 4.7 collective-permute-done.1
  382.4 4.7 collective-permute-done.1
  399.3 4.7 collective-permute-done.1
  433.2 4.7 collective-permute-done.1
  450.2 4.7 collective-permute-done.1
  484.1 4.7 collective-permute-done.1
  501.1 4.7 collective-permute-done.1
  535.0 4.7 collective-permute-done.1
  551.9 4.7 collective-permute-done.1
  580.6 9.8 %collective-permute-done.2 = f32[64,1152]{1,0:T(8,128)S(1)} collective-permute-done((f32[64,1152]{1,0:T(8,128)S(1)}, f32[64,1152]{1,0:T(8,128)S(1)}, u32[]{:S(2)}, u32[]{:S(2)}) %collective-permute-start.2) | collective-permute-done | bytes 294944 | tf_op jit(solution)/shard_map/ppermute | solution.py:12
  591.4 33.4 %reduce-scatter.2.cloned.1.call-done = f32[64,1152]{1,0:T(8,128)} async-done(((f32[512,1152]{1,0:T(8,128)}), f32[64,1152]{1,0:T(8,128)}) %reduce-scatter.2.cloned.1.call-update) | async-done | bytes 294928 | tf_op jit(solution)/shard_map/reduce_scatter | solution.py:89
  (506 shorter events, 442.9 us)
Async XLA Ops:
  7.2 44.0 %all-gather.2.cloned.1.call-start = ((), (), s32[]{:S(2)}) async-start(), calls=%async_computation.1 | async-start | bytes 1327104 | tf_op jit(solution)/shard_map/all_gather | solution.py:56
  10.0 614.9 %reduce-scatter.2.cloned.1.call-start = ((), (), s32[]{:S(2)}) async-start(), calls=%async_computation.2 | async-start | bytes 2654208 | tf_op jit(solution)/shard_map/reduce_scatter | solution.py:89
  53.6 13.0 %collective-permute-start = (bf16[64,1152]{1,0:T(8,128)(2,1)}, bf16[64,1152]{1,0:T(8,128)(2,1)}, u32[]{:S(2)}, u32[]{:S(2)}) collective-permute-start(bf16[64,1152]{1,0:T(8,128)(2,1)} %copy.11), channel_id=1, source_target_pairs={{248,0},{0,8},{8,16},{16,24},{24,32},{32,40},{40,48},{48,56},{56,6... | collective-permute-start | bytes 442376 | tf_op jit(solution)/shard_map/while/body/eval_jaxpr/ppermute | solution.py:12
  122.8 10.0 %collective-permute-start.1 = (f32[64,1152]{1,0:T(8,128)}, f32[64,1152]{1,0:T(8,128)S(1)}, u32[]{:S(2)}, u32[]{:S(2)}) collective-permute-start(f32[64,1152]{1,0:T(8,128)} %convolution_add_fusion.6), channel_id=1, source_target_pairs={{248,0},{0,8},{8,16},{16,24},{24,32},{32,40},{40,48},{48,56},{56,6... | collective-permute-start | bytes 884744 | tf_op jit(solution)/shard_map/while/body/eval_jaxpr/ppermute | solution.py:12
  139.7 10.0 %collective-permute-start.1 = (f32[64,1152]{1,0:T(8,128)}, f32[64,1152]{1,0:T(8,128)S(1)}, u32[]{:S(2)}, u32[]{:S(2)}) collective-permute-start(f32[64,1152]{1,0:T(8,128)} %convolution_add_fusion.6), channel_id=1, source_target_pairs={{248,0},{0,8},{8,16},{16,24},{24,32},{32,40},{40,48},{48,56},{56,6... | collective-permute-start | bytes 884744 | tf_op jit(solution)/shard_map/while/body/eval_jaxpr/ppermute | solution.py:12
  156.7 10.0 %collective-permute-start.1 = (f32[64,1152]{1,0:T(8,128)}, f32[64,1152]{1,0:T(8,128)S(1)}, u32[]{:S(2)}, u32[]{:S(2)}) collective-permute-start(f32[64,1152]{1,0:T(8,128)} %convolution_add_fusion.6), channel_id=1, source_target_pairs={{248,0},{0,8},{8,16},{16,24},{24,32},{32,40},{40,48},{48,56},{56,6... | collective-permute-start | bytes 884744 | tf_op jit(solution)/shard_map/while/body/eval_jaxpr/ppermute | solution.py:12
  173.6 10.0 %collective-permute-start.1 = (f32[64,1152]{1,0:T(8,128)}, f32[64,1152]{1,0:T(8,128)S(1)}, u32[]{:S(2)}, u32[]{:S(2)}) collective-permute-start(f32[64,1152]{1,0:T(8,128)} %convolution_add_fusion.6), channel_id=1, source_target_pairs={{248,0},{0,8},{8,16},{16,24},{24,32},{32,40},{40,48},{48,56},{56,6... | collective-permute-start | bytes 884744 | tf_op jit(solution)/shard_map/while/body/eval_jaxpr/ppermute | solution.py:12
  190.6 10.0 %collective-permute-start.1 = (f32[64,1152]{1,0:T(8,128)}, f32[64,1152]{1,0:T(8,128)S(1)}, u32[]{:S(2)}, u32[]{:S(2)}) collective-permute-start(f32[64,1152]{1,0:T(8,128)} %convolution_add_fusion.6), channel_id=1, source_target_pairs={{248,0},{0,8},{8,16},{16,24},{24,32},{32,40},{40,48},{48,56},{56,6... | collective-permute-start | bytes 884744 | tf_op jit(solution)/shard_map/while/body/eval_jaxpr/ppermute | solution.py:12
  207.5 10.0 %collective-permute-start.1 = (f32[64,1152]{1,0:T(8,128)}, f32[64,1152]{1,0:T(8,128)S(1)}, u32[]{:S(2)}, u32[]{:S(2)}) collective-permute-start(f32[64,1152]{1,0:T(8,128)} %convolution_add_fusion.6), channel_id=1, source_target_pairs={{248,0},{0,8},{8,16},{16,24},{24,32},{32,40},{40,48},{48,56},{56,6... | collective-permute-start | bytes 884744 | tf_op jit(solution)/shard_map/while/body/eval_jaxpr/ppermute | solution.py:12
  224.5 10.0 %collective-permute-start.1 = (f32[64,1152]{1,0:T(8,128)}, f32[64,1152]{1,0:T(8,128)S(1)}, u32[]{:S(2)}, u32[]{:S(2)}) collective-permute-start(f32[64,1152]{1,0:T(8,128)} %convolution_add_fusion.6), channel_id=1, source_target_pairs={{248,0},{0,8},{8,16},{16,24},{24,32},{32,40},{40,48},{48,56},{56,6... | collective-permute-start | bytes 884744 | tf_op jit(solution)/shard_map/while/body/eval_jaxpr/ppermute | solution.py:12
  241.4 10.0 %collective-permute-start.1 = (f32[64,1152]{1,0:T(8,128)}, f32[64,1152]{1,0:T(8,128)S(1)}, u32[]{:S(2)}, u32[]{:S(2)}) collective-permute-start(f32[64,1152]{1,0:T(8,128)} %convolution_add_fusion.6), channel_id=1, source_target_pairs={{248,0},{0,8},{8,16},{16,24},{24,32},{32,40},{40,48},{48,56},{56,6... | collective-permute-start | bytes 884744 | tf_op jit(solution)/shard_map/while/body/eval_jaxpr/ppermute | solution.py:12
  258.4 10.0 %collective-permute-start.1 = (f32[64,1152]{1,0:T(8,128)}, f32[64,1152]{1,0:T(8,128)S(1)}, u32[]{:S(2)}, u32[]{:S(2)}) collective-permute-start(f32[64,1152]{1,0:T(8,128)} %convolution_add_fusion.6), channel_id=1, source_target_pairs={{248,0},{0,8},{8,16},{16,24},{24,32},{32,40},{40,48},{48,56},{56,6... | collective-permute-start | bytes 884744 | tf_op jit(solution)/shard_map/while/body/eval_jaxpr/ppermute | solution.py:12
  275.3 10.0 %collective-permute-start.1 = (f32[64,1152]{1,0:T(8,128)}, f32[64,1152]{1,0:T(8,128)S(1)}, u32[]{:S(2)}, u32[]{:S(2)}) collective-permute-start(f32[64,1152]{1,0:T(8,128)} %convolution_add_fusion.6), channel_id=1, source_target_pairs={{248,0},{0,8},{8,16},{16,24},{24,32},{32,40},{40,48},{48,56},{56,6... | collective-permute-start | bytes 884744 | tf_op jit(solution)/shard_map/while/body/eval_jaxpr/ppermute | solution.py:12
  292.3 10.0 %collective-permute-start.1 = (f32[64,1152]{1,0:T(8,128)}, f32[64,1152]{1,0:T(8,128)S(1)}, u32[]{:S(2)}, u32[]{:S(2)}) collective-permute-start(f32[64,1152]{1,0:T(8,128)} %convolution_add_fusion.6), channel_id=1, source_target_pairs={{248,0},{0,8},{8,16},{16,24},{24,32},{32,40},{40,48},{48,56},{56,6... | collective-permute-start | bytes 884744 | tf_op jit(solution)/shard_map/while/body/eval_jaxpr/ppermute | solution.py:12
  326.2 10.0 %collective-permute-start.1 = (f32[64,1152]{1,0:T(8,128)}, f32[64,1152]{1,0:T(8,128)S(1)}, u32[]{:S(2)}, u32[]{:S(2)}) collective-permute-start(f32[64,1152]{1,0:T(8,128)} %convolution_add_fusion.6), channel_id=1, source_target_pairs={{248,0},{0,8},{8,16},{16,24},{24,32},{32,40},{40,48},{48,56},{56,6... | collective-permute-start | bytes 884744 | tf_op jit(solution)/shard_map/while/body/eval_jaxpr/ppermute | solution.py:12
  343.2 10.0 %collective-permute-start.1 = (f32[64,1152]{1,0:T(8,128)}, f32[64,1152]{1,0:T(8,128)S(1)}, u32[]{:S(2)}, u32[]{:S(2)}) collective-permute-start(f32[64,1152]{1,0:T(8,128)} %convolution_add_fusion.6), channel_id=1, source_target_pairs={{248,0},{0,8},{8,16},{16,24},{24,32},{32,40},{40,48},{48,56},{56,6... | collective-permute-start | bytes 884744 | tf_op jit(solution)/shard_map/while/body/eval_jaxpr/ppermute | solution.py:12
  377.1 10.0 %collective-permute-start.1 = (f32[64,1152]{1,0:T(8,128)}, f32[64,1152]{1,0:T(8,128)S(1)}, u32[]{:S(2)}, u32[]{:S(2)}) collective-permute-start(f32[64,1152]{1,0:T(8,128)} %convolution_add_fusion.6), channel_id=1, source_target_pairs={{248,0},{0,8},{8,16},{16,24},{24,32},{32,40},{40,48},{48,56},{56,6... | collective-permute-start | bytes 884744 | tf_op jit(solution)/shard_map/while/body/eval_jaxpr/ppermute | solution.py:12
  394.0 10.0 %collective-permute-start.1 = (f32[64,1152]{1,0:T(8,128)}, f32[64,1152]{1,0:T(8,128)S(1)}, u32[]{:S(2)}, u32[]{:S(2)}) collective-permute-start(f32[64,1152]{1,0:T(8,128)} %convolution_add_fusion.6), channel_id=1, source_target_pairs={{248,0},{0,8},{8,16},{16,24},{24,32},{32,40},{40,48},{48,56},{56,6... | collective-permute-start | bytes 884744 | tf_op jit(solution)/shard_map/while/body/eval_jaxpr/ppermute | solution.py:12
  427.9 10.0 %collective-permute-start.1 = (f32[64,1152]{1,0:T(8,128)}, f32[64,1152]{1,0:T(8,128)S(1)}, u32[]{:S(2)}, u32[]{:S(2)}) collective-permute-start(f32[64,1152]{1,0:T(8,128)} %convolution_add_fusion.6), channel_id=1, source_target_pairs={{248,0},{0,8},{8,16},{16,24},{24,32},{32,40},{40,48},{48,56},{56,6... | collective-permute-start | bytes 884744 | tf_op jit(solution)/shard_map/while/body/eval_jaxpr/ppermute | solution.py:12
  444.9 10.0 %collective-permute-start.1 = (f32[64,1152]{1,0:T(8,128)}, f32[64,1152]{1,0:T(8,128)S(1)}, u32[]{:S(2)}, u32[]{:S(2)}) collective-permute-start(f32[64,1152]{1,0:T(8,128)} %convolution_add_fusion.6), channel_id=1, source_target_pairs={{248,0},{0,8},{8,16},{16,24},{24,32},{32,40},{40,48},{48,56},{56,6... | collective-permute-start | bytes 884744 | tf_op jit(solution)/shard_map/while/body/eval_jaxpr/ppermute | solution.py:12
  478.8 10.0 %collective-permute-start.1 = (f32[64,1152]{1,0:T(8,128)}, f32[64,1152]{1,0:T(8,128)S(1)}, u32[]{:S(2)}, u32[]{:S(2)}) collective-permute-start(f32[64,1152]{1,0:T(8,128)} %convolution_add_fusion.6), channel_id=1, source_target_pairs={{248,0},{0,8},{8,16},{16,24},{24,32},{32,40},{40,48},{48,56},{56,6... | collective-permute-start | bytes 884744 | tf_op jit(solution)/shard_map/while/body/eval_jaxpr/ppermute | solution.py:12
  495.8 10.0 %collective-permute-start.1 = (f32[64,1152]{1,0:T(8,128)}, f32[64,1152]{1,0:T(8,128)S(1)}, u32[]{:S(2)}, u32[]{:S(2)}) collective-permute-start(f32[64,1152]{1,0:T(8,128)} %convolution_add_fusion.6), channel_id=1, source_target_pairs={{248,0},{0,8},{8,16},{16,24},{24,32},{32,40},{40,48},{48,56},{56,6... | collective-permute-start | bytes 884744 | tf_op jit(solution)/shard_map/while/body/eval_jaxpr/ppermute | solution.py:12
  529.7 10.0 %collective-permute-start.1 = (f32[64,1152]{1,0:T(8,128)}, f32[64,1152]{1,0:T(8,128)S(1)}, u32[]{:S(2)}, u32[]{:S(2)}) collective-permute-start(f32[64,1152]{1,0:T(8,128)} %convolution_add_fusion.6), channel_id=1, source_target_pairs={{248,0},{0,8},{8,16},{16,24},{24,32},{32,40},{40,48},{48,56},{56,6... | collective-permute-start | bytes 884744 | tf_op jit(solution)/shard_map/while/body/eval_jaxpr/ppermute | solution.py:12
  546.6 10.0 %collective-permute-start.1 = (f32[64,1152]{1,0:T(8,128)}, f32[64,1152]{1,0:T(8,128)S(1)}, u32[]{:S(2)}, u32[]{:S(2)}) collective-permute-start(f32[64,1152]{1,0:T(8,128)} %convolution_add_fusion.6), channel_id=1, source_target_pairs={{248,0},{0,8},{8,16},{16,24},{24,32},{32,40},{40,48},{48,56},{56,6... | collective-permute-start | bytes 884744 | tf_op jit(solution)/shard_map/while/body/eval_jaxpr/ppermute | solution.py:12
  (138 other events, 678.6 us)
Sparse Core Ops, SparseCore 0:
  10.4 40.8 all-gather.1
  579.0 45.7 reduce-scatter.1
where the time goes:
time: 641 us; the launch traced here: 635 us
  waiting for transfers between devices  317 us (49%)
  matrix products  202 us (32%)
  local copies, waits for them, and re-layouts  76.4 us (12%)
  between operations  15.5 us (2%)
  starting transfers between devices  11.7 us (2%)
  other arithmetic  10.2 us (2%)
    ppermute x63, waiting for transfers between devices, from_behind(): return lax.ppermute(block, axis, route)  247 us
    dot_general x32, matrix products, coef_of(): lax.dot_general(q_rows, p_rows, (((1,), (1,)), ((), ())), preferred_eleme...  79.8 us
    while x217, local copies, waits for them, and re-layouts  74.3 us
    dot_general x32, matrix products, block_terms(): grad_q = jnp.dot(coef, p_all, preferred_element_type=jnp.float32)  63.2 us
    dot_general x32, matrix products, block_terms(): lax.dot_general(coef, q_blk, (((0,), (0,)), ((), ())), preferred_element_...  59.5 us
    all_gather x1, waiting for transfers between devices, on_device(): p_all = lax.all_gather(p_own, 'mp', axis=0, tiled=True)  36.5 us
    reduce_scatter x1, waiting for transfers between devices, on_device(): image_part = lax.psum_scatter(grad_p, 'mp', scatter_dimension=0, tiled=True)  33.4 us
  transfers between devices with their start and end apart: 65, of which 63 were waited for; matrix products, arithmetic and copies ran while one was open for 32% of the time, Pallas kernels for 0%

commit v1 on v0

v1 whole, which is shorter than its diff:
```python
import functools

import jax
import jax.numpy as jnp
from jax import lax
from jax.experimental import pallas as pl
from jax.experimental.pallas import tpu as pltpu
from jax.sharding import PartitionSpec as P

EPS = 1e-06
MESH = pl.DeviceIdType.MESH
NX, NY, NZ = 4, 4, 8
ROWS = 64
HALF = ROWS // 2
QUARTER = ROWS // 4
NT = (((1,), (1,)), ((), ()))
TN = (((0,), (0,)), ((), ()))
NN = (((1,), (0,)), ((), ()))

IMG_SLOTS = [
    (0, 0), (1, 0), (3, 0), (0, 1), (0, 3), (2, 0),
    (1, 1), (1, 3), (3, 1), (3, 3), (0, 2), (2, 1),
    (2, 3), (1, 2), (3, 2), (2, 2),
]
TXT_SLOTS = [(dz, s) for dz in (0, 1, 7, 2, 6, 3, 5, 4) for s in (0, 1)]


class Edge:
    def __init__(self, src, dst, row, count, axis, sign):
        self.src, self.dst, self.row, self.count = src, dst, row, count
        self.axis, self.sign = axis, sign


def img_edges():
    edges = {}
    for half, first, second in (("A", "x", "y"), ("B", "y", "x")):
        base = 0 if half == "A" else HALF

        def at(df, ds, first=first):
            return (df % 4, ds % 4) if first == "x" else (ds % 4, df % 4)

        for sg in (1, -1):
            quarter = base + (0 if sg == 1 else QUARTER)
            edges[half, "f", sg] = Edge(at(0, 0), at(-sg, 0), base, HALF, first, sg)
            edges[half, "fq", sg] = Edge(at(-sg, 0), at(2, 0), quarter, QUARTER, first, sg)
            for df in range(4):
                edges[half, "s", df, sg] = Edge(at(df, 0), at(df, -sg), base, HALF, second, sg)
                edges[half, "sq", df, sg] = Edge(at(df, -sg), at(df, 2), quarter, QUARTER, second, sg)
    return edges


def txt_edges():
    edges = {}
    for sg in (1, -1):
        for k in range(3):
            edges["z", k, sg] = Edge(((-sg * k) % NZ, 0), ((-sg * (k + 1)) % NZ, 0), 0, ROWS, "z", sg)
        edges["z", 3, sg] = Edge(
            ((-sg * 3) % NZ, 0), (4, 0), 0 if sg == 1 else HALF, HALF, "z", sg
        )
    for dz in range(NZ):
        edges["c", dz] = Edge((dz, 0), (dz, 1), 0, ROWS, "c", 1)
    return edges


class Side:
    def __init__(self, slots, edges, rows, part, out, back, sems, place):
        self.at = {slot: i * ROWS for i, slot in enumerate(slots)}
        self.edges = edges
        self.number = {key: i for i, key in enumerate(edges)}
        self.rows, self.part, self.out, self.back = rows, part, out, back
        self.g_send, self.g_recv, self.r_send, self.r_recv = sems
        self.place = place
        self.sent, self.returned = set(), set()
        self.seen, self.taken = set(), set()

    def span(self, slot, row, count):
        return pl.ds(self.at[slot] + row, count)

    def gather_copy(self, key):
        e, i = self.edges[key], self.number[key]
        return pltpu.make_async_remote_copy(
            src_ref=self.rows.at[self.span(e.src, e.row, e.count)],
            dst_ref=self.rows.at[self.span(e.dst, e.row, e.count)],
            send_sem=self.g_send.at[i],
            recv_sem=self.g_recv.at[i],
            device_id=self.place(e.axis, e.sign),
            device_id_type=MESH,
        )

    def scatter_copy(self, key):
        e, i = self.edges[key], self.number[key]
        where = self.span(e.dst, e.row, e.count)
        return pltpu.make_async_remote_copy(
            src_ref=self.out.at[where],
            dst_ref=self.back.at[where],
            send_sem=self.r_send.at[i],
            recv_sem=self.r_recv.at[i],
            device_id=self.place(e.axis, -e.sign),
            device_id_type=MESH,
        )

    def send(self, *keys):
        for key in keys:
            e = self.edges[key]
            self.arrive(e.src, e.row, e.count)
            self.gather_copy(key).start()
            self.sent.add(key)

    def arrive(self, slot, row=0, count=ROWS):
        for key, e in self.edges.items():
            if e.dst == slot and e.row < row + count and row < e.row + e.count and key not in self.seen:
                assert key in self.sent, key
                self.gather_copy(key).wait_recv()
                self.seen.add(key)

    def total(self, slot, row, count):
        value = self.part[self.span(slot, row, count), :]
        for key, e in self.edges.items():
            if e.src == slot and e.row <= row and row + count <= e.row + e.count:
                if key not in self.taken:
                    assert key in self.returned, key
                    self.scatter_copy(key).wait_recv()
                    self.taken.add(key)
                value = value + self.back[self.span(e.dst, row, count), :].astype(jnp.float32)
        return value

    def give(self, *keys):
        for key in keys:
            e = self.edges[key]
            for row in range(e.row, e.row + e.count, QUARTER):
                self.out[self.span(e.dst, row, QUARTER), :] = self.total(e.dst, row, QUARTER).astype(jnp.bfloat16)
            self.scatter_copy(key).start()
            self.returned.add(key)

    def finish(self):
        assert len(self.sent) == len(self.returned) == len(self.seen) == len(self.taken) == len(self.edges)
        for key in self.edges:
            self.gather_copy(key).wait_send()
            self.scatter_copy(key).wait_send()


def unit_of(emb):
    wide = emb.astype(jnp.float32)
    inverse = lax.rsqrt(jnp.sum(wide * wide, axis=1, keepdims=True) + EPS)
    return wide * inverse, inverse


def back_norm(unit, inverse, grad):
    return inverse * (grad - unit * jnp.sum(unit * grad, axis=1, keepdims=True))


def kernel(
    img_ref, txt_ref, temp_ref, bias_ref, img_out, txt_out,
    p_rows, q_rows, coef, p_part, q_part, p_send, q_send, p_back, q_back,
    pg_send, pg_recv, pr_send, pr_recv, qg_send, qg_recv, qr_send, qr_recv,
):
    dp, mp = lax.axis_index("dp"), lax.axis_index("mp")
    core, z, x = dp % 2, (dp // 2) % NZ, (dp // (2 * NZ)) * 2 + mp // NY
    y = mp % NY

    def place(axis, sign):
        nx, ny, nz, nc = x, y, z, core
        if axis == "x":
            nx = (x + sign + NX) % NX
        elif axis == "y":
            ny = (y + sign + NY) % NY
        elif axis == "z":
            nz = (z + sign + NZ) % NZ
        else:
            nc = 1 - core
        return ((nx // 2) * (2 * NZ) + nz * 2 + nc, (nx % 2) * NY + ny)

    barrier = pltpu.get_barrier_semaphore()
    neighbours = [place(a, s) for a in "xyz" for s in (1, -1)] + [place("c", 1)]
    for device in neighbours:
        pl.semaphore_signal(barrier, inc=1, device_id=device, device_id_type=MESH)

    img = Side(IMG_SLOTS, img_edges(), p_rows, p_part, p_send, p_back,
               (pg_send, pg_recv, pr_send, pr_recv), place)
    txt = Side(TXT_SLOTS, txt_edges(), q_rows, q_part, q_send, q_back,
               (qg_send, qg_recv, qr_send, qr_recv), place)

    half_tau = 0.5 * jnp.exp(jnp.full((1, 1), temp_ref[0], jnp.float32))
    half_bias = 0.5 * jnp.full((1, 1), bias_ref[0], jnp.float32)

    p_rows[0:ROWS, :] = unit_of(img_ref[...])[0].astype(jnp.bfloat16)
    q_rows[0:ROWS, :] = unit_of(txt_ref[...])[0].astype(jnp.bfloat16)
    pl.semaphore_wait(barrier, len(neighbours))

    def scores(t0, tn, i0, n):
        dots = lax.dot_general(q_rows[t0:t0 + tn, :], p_rows[i0:i0 + n, :], NT,
                               preferred_element_type=jnp.float32)
        wave = jnp.tanh(half_tau * dots + half_bias)
        coef[t0:t0 + tn, i0:i0 + n] = (half_tau * wave + half_tau).astype(jnp.bfloat16)

    def own_scores():
        dots = lax.dot_general(q_rows[0:ROWS, :], p_rows[0:128, :], NT,
                               preferred_element_type=jnp.float32)
        wave = jnp.tanh(half_tau * dots + half_bias)
        same = lax.broadcasted_iota(jnp.int32, dots.shape, 0) == lax.broadcasted_iota(jnp.int32, dots.shape, 1)
        coef[0:ROWS, 0:128] = (half_tau * wave + jnp.where(same, -half_tau, half_tau)).astype(jnp.bfloat16)

    def img_grads(i0, n):
        p_part[i0:i0 + n, :] = lax.dot_general(coef[:, i0:i0 + n], q_rows[...], TN,
                                               preferred_element_type=jnp.float32)

    def txt_grads(t0, n):
        q_part[t0:t0 + n, :] = lax.dot_general(coef[t0:t0 + n, :], p_rows[...], NN,
                                               preferred_element_type=jnp.float32)

    both = (1, -1)
    for sg in both:
        img.send(("A", "f", sg))
        img.send(("B", "f", sg))
        txt.send(("z", 0, sg))
    for sg in both:
        img.send(("A", "s", 0, sg))
        img.send(("B", "s", 0, sg))
    txt.send(("c", 0))
    for sg in both:
        for half in "AB":
            img.send((half, "fq", sg))
            img.send((half, "s", -sg % 4, 1), (half, "s", -sg % 4, -1))
    for sg in both:
        txt.send(("z", 1, sg))
        txt.send(("c", -sg % NZ))
    for sg in both:
        for half in "AB":
            img.send((half, "sq", 0, sg))
    for half in "AB":
        for sg in both:
            img.send((half, "s", 2, sg))
    for slot in IMG_SLOTS[:6]:
        img.arrive(slot)
    for slot in TXT_SLOTS[:6]:
        txt.arrive(slot)
    scores(0, 384, 0, 384)
    own_scores()
    for sg in both:
        txt.send(("z", 2, sg))
        txt.send(("c", -2 * sg % NZ))
    for df in (1, 3):
        for sg in both:
            for half in "AB":
                img.send((half, "sq", df, sg))
    for slot in TXT_SLOTS[6:10]:
        txt.arrive(slot)
    scores(384, 256, 0, 384)
    for sg in both:
        txt.send(("z", 3, sg))
        txt.send(("c", -3 * sg % NZ))
    for sg in both:
        for half in "AB":
            img.send((half, "sq", 2, sg))
    for slot in IMG_SLOTS[6:12]:
        img.arrive(slot)
    scores(0, 640, 384, 384)
    for slot in TXT_SLOTS[10:14]:
        txt.arrive(slot)
    scores(640, 256, 0, 768)
    txt.send(("c", 4))
    for slot in IMG_SLOTS[12:]:
        img.arrive(slot)
    scores(0, 896, 768, 256)
    for slot in TXT_SLOTS[14:]:
        txt.arrive(slot)
    scores(896, 128, 0, 1024)

    img_grads(768, 256)
    for half in "AB":
        for sg in both:
            img.give((half, "sq", 2, sg))
    for sg in both:
        img.give(("A", "sq", 1, sg), ("A", "sq", 3, sg))
    for sg in both:
        img.give(("B", "sq", 3, sg))
    txt_grads(640, 384)
    for dz in (4, 3, 5):
        txt.give(("c", dz))
    img_grads(384, 384)
    for sg in both:
        img.give(("B", "sq", 1, sg), ("A", "sq", 0, sg))
    for sg in both:
        txt.give(("z", 3, sg))
    for half in "AB":
        for sg in both:
            img.give((half, "s", 2, sg))
    txt_grads(384, 256)
    for dz in (2, 6):
        txt.give(("c", dz))
    for half in "AB":
        for sg in both:
            img.give((half, "s", 1, sg), (half, "s", 3, sg))
    for sg in both:
        txt.give(("z", 2, sg))
    img_grads(0, 384)
    for sg in both:
        img.give(("B", "sq", 0, sg))
    for half in "AB":
        for sg in both:
            img.give((half, "fq", sg))
    txt_grads(0, 384)
    for dz in (1, 7, 0):
        txt.give(("c", dz))
    for sg in both:
        txt.give(("z", 1, sg))
    for half in "AB":
        for sg in both:
            img.give((half, "s", 0, sg))
    for half in "AB":
        for sg in both:
            img.give((half, "f", sg))
    for sg in both:
        txt.give(("z", 0, sg))

    for side, ref, out in ((img, img_ref, img_out), (txt, txt_ref, txt_out)):
        for row in range(0, ROWS, QUARTER):
            unit, inverse = unit_of(ref[row:row + QUARTER, :])
            out[row:row + QUARTER, :] = back_norm(unit, inverse, side.total((0, 0), row, QUARTER))
    img.finish()
    txt.finish()


def on_device(image_emb, text_emb, log_temp, bias):
    rows, width = image_emb.shape
    group = 16 * rows
    n_img, n_txt = len(img_edges()), len(txt_edges())
    vmem = pl.BlockSpec(memory_space=pltpu.VMEM)
    smem = pl.BlockSpec(memory_space=pltpu.SMEM)
    return pl.pallas_call(
        kernel,
        out_shape=[jax.ShapeDtypeStruct((rows, width), jnp.float32)] * 2,
        in_specs=[vmem, vmem, smem, smem],
        out_specs=[vmem, vmem],
        scratch_shapes=(
            [pltpu.VMEM((group, width), jnp.bfloat16)] * 2
            + [pltpu.VMEM((group, group), jnp.bfloat16)]
            + [pltpu.VMEM((group, width), jnp.float32)] * 2
            + [pltpu.VMEM((group, width), jnp.bfloat16)] * 4
            + [pltpu.SemaphoreType.DMA((n_img,))] * 4
            + [pltpu.SemaphoreType.DMA((n_txt,))] * 4
        ),
        compiler_params=pltpu.CompilerParams(
            collective_id=0, has_side_effects=True, vmem_limit_bytes=56 * 2**20
        ),
    )(image_emb, text_emb, log_temp, bias)


def solution(mesh):
    placed = (P(("dp", "mp"), None), P(("dp", "mp"), None), P(), P())
    return jax.shard_map(
        on_device,
        mesh=mesh,
        in_specs=placed,
        out_specs=(P(("dp", "mp"), None), P(("dp", "mp"), None)),
        check_vma=False,
    )
```

time: 641 us -> 60.4 us (0.09)
  waiting for transfers between devices: 317 us -> 0 us
  matrix products: 202 us -> 0 us
  local copies, waits for them, and re-layouts: 76.4 us -> 2.46 us
  Pallas kernels: 0 us -> 54.9 us
  between operations: 15.5 us -> 1.94 us
  starting transfers between devices: 11.7 us -> 0 us
  other arithmetic: 10.2 us -> 0 us
    ppermute x63 -> x0, waiting for transfers between devices: 247 us -> none  [from_behind(): return lax.ppermute(block, axis, route)]
    dot_general x96 -> x0, matrix products: 202 us -> none  [the longest x32 79.8 us: coef_of(): lax.dot_general(q_rows, p_rows, (((1,), (1,)), ((), ())), preferred_eleme...]
    while x217 -> x0, local copies, waits for them, and re-layouts: 74.3 us -> none
    pallas_call x0 -> x1, Pallas kernels: none -> 54.9 us  [on_device(): pl.pallas_call(kernel, out_shape=[jax.ShapeDtypeStruct((rows, width), jnp...]
    all_gather x1 -> x0, waiting for transfers between devices: 36.5 us -> none  [on_device(): p_all = lax.all_gather(p_own, 'mp', axis=0, tiled=True)]
    reduce_scatter x1 -> x0, waiting for transfers between devices: 33.4 us -> none  [on_device(): image_part = lax.psum_scatter(grad_p, 'mp', scatter_dimension=0, tiled=True)]
    ppermute x63 -> x0, starting transfers between devices: 11.6 us -> none  [from_behind(): return lax.ppermute(block, axis, route)]
  transfers between devices with their start and end apart: 65 -> 0, of which waited for: 63 -> 0; matrix products, arithmetic and copies ran while one was open for 32% -> 0% of each run, Pallas kernels for 0% -> 0%
where the time goes in v1:
time: 60.4 us; the launch traced here: 59.2 us
  Pallas kernels  54.9 us (91%)
  local copies, waits for them, and re-layouts  2.46 us (4%)
  between operations  1.94 us (3%)
    pallas_call x1, Pallas kernels, on_device(): pl.pallas_call(kernel, out_shape=[jax.ShapeDtypeStruct((rows, width), jnp...  54.9 us
    unnamed x4, local copies, waits for them, and re-layouts  2.46 us

profile of v1, /device:TPU:1, one launch (start us, length us, event | category | flops | bytes accessed | tf_op | source)
XLA Modules:
  0.0 59.2 jit_solution(8884566193779255017)
XLA Ops:
  1.9 54.9 %shard_map.59 = (f32[64,1152]{1,0:T(8,128)}, f32[64,1152]{1,0:T(8,128)}) custom-call(bf16[64,1152]{1,0:T(8,128)(2,1)} %img_ref.1, bf16[64,1152]{1,0:T(8,128)(2,1)} %txt_ref.1, f32[1]{0:T(128)S(6)} %copy.8.temp_ref, f32[1]{0:T(128)S(6)} %copy.9.bias_ref), custom_call_target="tpu_custom_call" | custom-call | tf_op jit(solution)/shard_map/pallas_call | solution.py:330
  56.8 0.0 copy-start
  56.8 1.7 %copy.10 = f32[64,1152]{1,0:T(8,128)} copy(f32[64,1152]{1,0:T(8,128)} %get-tuple-element.4) | data formatting | bytes 589824
  58.5 0.0 copy-done
  58.5 0.7 %copy.11 = f32[64,1152]{1,0:T(8,128)} copy(f32[64,1152]{1,0:T(8,128)S(1)} %copy-done) | data formatting | bytes 589824
Async XLA Ops:
  56.8 1.8 %copy-start = (f32[64,1152]{1,0:T(8,128)S(1)}, f32[64,1152]{1,0:T(8,128)}, u32[]{:S(2)}) copy-start(f32[64,1152]{1,0:T(8,128)} %get-tuple-element.5) | copy-start | bytes 884740

commit v2 on v1

--- a/solution.py
+++ b/solution.py
@@ -16,13 +16,20 @@
 NT = (((1,), (1,)), ((), ()))
 TN = (((0,), (0,)), ((), ()))
 NN = (((1,), (0,)), ((), ()))
-
-IMG_SLOTS = [
-    (0, 0), (1, 0), (3, 0), (0, 1), (0, 3), (2, 0),
-    (1, 1), (1, 3), (3, 1), (3, 3), (0, 2), (2, 1),
-    (2, 3), (1, 2), (3, 2), (2, 2),
-]
-TXT_SLOTS = [(dz, s) for dz in (0, 1, 7, 2, 6, 3, 5, 4) for s in (0, 1)]
+CHUNKS = {1: (0, 1, 2, 3), -1: (2, 3, 0, 1)}
+
+IMG_UNITS = (
+    [((0, 0), 0), ((0, 0), 1)]
+    + [((d, 0), 0) for d in (1, 3)] + [((0, d), 1) for d in (1, 3)]
+    + [((0, d), 0) for d in (1, 3)] + [((d, 0), 1) for d in (1, 3)]
+    + [((2, 0), 0), ((0, 2), 1)]
+    + [((3, d), 0) for d in (1, 3)] + [((d, 3), 1) for d in (1, 3)]
+    + [((0, 2), 0), ((2, 0), 1)]
+    + [((1, d), 0) for d in (1, 3)] + [((d, 1), 1) for d in (1, 3)]
+    + [((2, d), 0) for d in (1, 3)] + [((d, 2), 1) for d in (1, 3)]
+    + [((3, 2), 0), ((2, 3), 1), ((1, 2), 0), ((2, 1), 1), ((2, 2), 0), ((2, 2), 1)]
+)
+TXT_UNITS = [((dz, s), 0) for dz in (0, 1, 7, 2, 6, 3, 5, 4) for s in (0, 1)]
 
 
 class Edge:
@@ -52,19 +59,21 @@
 def txt_edges():
     edges = {}
     for sg in (1, -1):
-        for k in range(3):
-            edges["z", k, sg] = Edge(((-sg * k) % NZ, 0), ((-sg * (k + 1)) % NZ, 0), 0, ROWS, "z", sg)
-        edges["z", 3, sg] = Edge(
-            ((-sg * 3) % NZ, 0), (4, 0), 0 if sg == 1 else HALF, HALF, "z", sg
-        )
+        for k in range(4):
+            for c in CHUNKS[sg][: 4 if k < 3 else 2]:
+                edges["z", k, sg, c] = Edge(
+                    ((-sg * k) % NZ, 0), ((-sg * (k + 1)) % NZ, 0), c * QUARTER, QUARTER, "z", sg
+                )
     for dz in range(NZ):
         edges["c", dz] = Edge((dz, 0), (dz, 1), 0, ROWS, "c", 1)
     return edges
 
 
 class Side:
-    def __init__(self, slots, edges, rows, part, out, back, sems, place):
-        self.at = {slot: i * ROWS for i, slot in enumerate(slots)}
+    def __init__(self, units, edges, rows, part, out, back, sems, place):
+        self.unit = 16 * ROWS // len(units)
+        self.at = {unit: i * self.unit for i, unit in enumerate(units)}
+        self.done = set()
         self.edges = edges
         self.number = {key: i for i, key in enumerate(edges)}
         self.rows, self.part, self.out, self.back = rows, part, out, back
@@ -74,7 +83,7 @@
         self.seen, self.taken = set(), set()
 
     def span(self, slot, row, count):
-        return pl.ds(self.at[slot] + row, count)
+        return pl.ds(self.at[slot, row // self.unit] + row % self.unit, count)
 
     def gather_copy(self, key):
         e, i = self.edges[key], self.number[key]
@@ -106,6 +115,11 @@
             self.gather_copy(key).start()
             self.sent.add(key)
 
+    def arrive_until(self, end):
+        for (slot, which), start in self.at.items():
+            if start < end:
+                self.arrive(slot, which * self.unit, self.unit)
+
     def arrive(self, slot, row=0, count=ROWS):
         for key, e in self.edges.items():
             if e.dst == slot and e.row < row + count and row < e.row + e.count and key not in self.seen:
@@ -114,6 +128,7 @@
                 self.seen.add(key)
 
     def total(self, slot, row, count):
+        assert self.span(slot, row, count).start in self.done
         value = self.part[self.span(slot, row, count), :]
         for key, e in self.edges.items():
             if e.src == slot and e.row <= row and row + count <= e.row + e.count:
@@ -150,10 +165,19 @@
 
 
 def kernel(
-    img_ref, txt_ref, temp_ref, bias_ref, img_out, txt_out,
+    img_hbm, txt_hbm, temp_hbm, bias_hbm, img_out, txt_out,
+    img_ref, txt_ref, temp_ref, bias_ref, in_sems,
     p_rows, q_rows, coef, p_part, q_part, p_send, q_send, p_back, q_back,
     pg_send, pg_recv, pr_send, pr_recv, qg_send, qg_recv, qr_send, qr_recv,
 ):
+    loads = [
+        pltpu.make_async_copy(here, there, in_sems.at[i])
+        for i, (here, there) in enumerate(
+            ((img_hbm, img_ref), (txt_hbm, txt_ref), (temp_hbm, temp_ref), (bias_hbm, bias_ref))
+        )
+    ]
+    for load in loads:
+        load.start()
     dp, mp = lax.axis_index("dp"), lax.axis_index("mp")
     core, z, x = dp % 2, (dp // 2) % NZ, (dp // (2 * NZ)) * 2 + mp // NY
     y = mp % NY
@@ -175,19 +199,23 @@
     for device in neighbours:
         pl.semaphore_signal(barrier, inc=1, device_id=device, device_id_type=MESH)
 
-    img = Side(IMG_SLOTS, img_edges(), p_rows, p_part, p_send, p_back,
+    img = Side(IMG_UNITS, img_edges(), p_rows, p_part, p_send, p_back,
                (pg_send, pg_recv, pr_send, pr_recv), place)
-    txt = Side(TXT_SLOTS, txt_edges(), q_rows, q_part, q_send, q_back,
+    txt = Side(TXT_UNITS, txt_edges(), q_rows, q_part, q_send, q_back,
                (qg_send, qg_recv, qr_send, qr_recv), place)
 
-    half_tau = 0.5 * jnp.exp(jnp.full((1, 1), temp_ref[0], jnp.float32))
-    half_bias = 0.5 * jnp.full((1, 1), bias_ref[0], jnp.float32)
+    for load in loads:
+        load.wait()
+    half_tau = 0.5 * jnp.exp(temp_ref[...].reshape(1, 1))
+    half_bias = 0.5 * bias_ref[...].reshape(1, 1)
 
     p_rows[0:ROWS, :] = unit_of(img_ref[...])[0].astype(jnp.bfloat16)
     q_rows[0:ROWS, :] = unit_of(txt_ref[...])[0].astype(jnp.bfloat16)
     pl.semaphore_wait(barrier, len(neighbours))
 
     def scores(t0, tn, i0, n):
+        txt.arrive_until(t0 + tn)
+        img.arrive_until(i0 + n)
         dots = lax.dot_general(q_rows[t0:t0 + tn, :], p_rows[i0:i0 + n, :], NT,
                                preferred_element_type=jnp.float32)
         wave = jnp.tanh(half_tau * dots + half_bias)
@@ -201,117 +229,97 @@
         coef[0:ROWS, 0:128] = (half_tau * wave + jnp.where(same, -half_tau, half_tau)).astype(jnp.bfloat16)
 
     def img_grads(i0, n):
+        img.done.update(range(i0, i0 + n, QUARTER))
         p_part[i0:i0 + n, :] = lax.dot_general(coef[:, i0:i0 + n], q_rows[...], TN,
                                                preferred_element_type=jnp.float32)
 
     def txt_grads(t0, n):
+        txt.done.update(range(t0, t0 + n, QUARTER))
         q_part[t0:t0 + n, :] = lax.dot_general(coef[t0:t0 + n, :], p_rows[...], NN,
                                                preferred_element_type=jnp.float32)
 
     both = (1, -1)
-    for sg in both:
-        img.send(("A", "f", sg))
-        img.send(("B", "f", sg))
-        txt.send(("z", 0, sg))
-    for sg in both:
-        img.send(("A", "s", 0, sg))
-        img.send(("B", "s", 0, sg))
+
+    def ring(k, *places):
+        for i in places:
+            for sg in both:
+                txt.send(("z", k, sg, CHUNKS[sg][i]))
+
+    def ring_back(k, *places):
+        for i in places:
+            for sg in both:
+                txt.give(("z", k, sg, CHUNKS[sg][i]))
+
+    def across(kind, *far, way=img.send):
+        for df in far:
+            for half in "AB":
+                for sg in both:
+                    way((half, kind, df, sg))
+
+    def along(kind, way=img.send):
+        for half in "AB":
+            for sg in both:
+                way((half, kind, sg))
+
+    along("f")
+    ring(0, 0, 1, 2, 3)
+    across("s", 0)
     txt.send(("c", 0))
-    for sg in both:
-        for half in "AB":
-            img.send((half, "fq", sg))
-            img.send((half, "s", -sg % 4, 1), (half, "s", -sg % 4, -1))
-    for sg in both:
-        txt.send(("z", 1, sg))
-        txt.send(("c", -sg % NZ))
-    for sg in both:
-        for half in "AB":
-            img.send((half, "sq", 0, sg))
-    for half in "AB":
-        for sg in both:
-            img.send((half, "s", 2, sg))
-    for slot in IMG_SLOTS[:6]:
-        img.arrive(slot)
-    for slot in TXT_SLOTS[:6]:
-        txt.arrive(slot)
+    ring(1, 0)
+    along("fq")
+    across("s", 3)
+    ring(1, 1, 2)
+    across("sq", 0)
+    ring(1, 3)
+    txt.send(("c", 1), ("c", 7))
+    across("s", 1)
+    ring(2, 0)
+    across("s", 2)
+    ring(2, 1)
     scores(0, 384, 0, 384)
     own_scores()
-    for sg in both:
-        txt.send(("z", 2, sg))
-        txt.send(("c", -2 * sg % NZ))
-    for df in (1, 3):
-        for sg in both:
-            for half in "AB":
-                img.send((half, "sq", df, sg))
-    for slot in TXT_SLOTS[6:10]:
-        txt.arrive(slot)
+    ring(2, 2)
+    across("sq", 3)
+    ring(2, 3)
+    txt.send(("c", 2), ("c", 6))
+    ring(3, 0)
     scores(384, 256, 0, 384)
-    for sg in both:
-        txt.send(("z", 3, sg))
-        txt.send(("c", -3 * sg % NZ))
-    for sg in both:
-        for half in "AB":
-            img.send((half, "sq", 2, sg))
-    for slot in IMG_SLOTS[6:12]:
-        img.arrive(slot)
-    scores(0, 640, 384, 384)
-    for slot in TXT_SLOTS[10:14]:
-        txt.arrive(slot)
-    scores(640, 256, 0, 768)
+    ring(3, 1)
+    across("sq", 1)
+    scores(0, 640, 384, 256)
+    txt.send(("c", 3), ("c", 5))
+    across("sq", 2)
     txt.send(("c", 4))
-    for slot in IMG_SLOTS[12:]:
-        img.arrive(slot)
-    scores(0, 896, 768, 256)
-    for slot in TXT_SLOTS[14:]:
-        txt.arrive(slot)
+    scores(640, 256, 0, 640)
+    scores(0, 896, 640, 256)
+    scores(0, 896, 896, 128)
     scores(896, 128, 0, 1024)
 
+    txt_grads(896, 128)
+    txt.give(("c", 4))
     img_grads(768, 256)
-    for half in "AB":
-        for sg in both:
-            img.give((half, "sq", 2, sg))
-    for sg in both:
-        img.give(("A", "sq", 1, sg), ("A", "sq", 3, sg))
-    for sg in both:
-        img.give(("B", "sq", 3, sg))
-    txt_grads(640, 384)
-    for dz in (4, 3, 5):
-        txt.give(("c", dz))
-    img_grads(384, 384)
-    for sg in both:
-        img.give(("B", "sq", 1, sg), ("A", "sq", 0, sg))
-    for sg in both:
-        txt.give(("z", 3, sg))
-    for half in "AB":
-        for sg in both:
-            img.give((half, "s", 2, sg))
+    across("sq", 2, 3, 1, way=img.give)
+    txt_grads(640, 256)
+    txt.give(("c", 3), ("c", 5))
+    ring_back(3, 0, 1)
+    img_grads(512, 256)
+    across("sq", 0, way=img.give)
+    ring_back(2, 2, 3)
+    across("s", 2, way=img.give)
     txt_grads(384, 256)
-    for dz in (2, 6):
-        txt.give(("c", dz))
-    for half in "AB":
-        for sg in both:
-            img.give((half, "s", 1, sg), (half, "s", 3, sg))
-    for sg in both:
-        txt.give(("z", 2, sg))
-    img_grads(0, 384)
-    for sg in both:
-        img.give(("B", "sq", 0, sg))
-    for half in "AB":
-        for sg in both:
-            img.give((half, "fq", sg))
+    txt.give(("c", 2), ("c", 6))
+    ring_back(2, 0, 1)
+    img_grads(256, 256)
+    across("s", 3, 1, way=img.give)
+    ring_back(1, 2, 3)
     txt_grads(0, 384)
-    for dz in (1, 7, 0):
-        txt.give(("c", dz))
-    for sg in both:
-        txt.give(("z", 1, sg))
-    for half in "AB":
-        for sg in both:
-            img.give((half, "s", 0, sg))
-    for half in "AB":
-        for sg in both:
-            img.give((half, "f", sg))
-    for sg in both:
-        txt.give(("z", 0, sg))
+    txt.give(("c", 1), ("c", 7), ("c", 0))
+    ring_back(1, 0, 1)
+    img_grads(0, 256)
+    along("fq", way=img.give)
+    across("s", 0, way=img.give)
+    ring_back(0, 2, 3, 0, 1)
+    along("f", way=img.give)
 
     for side, ref, out in ((img, img_ref, img_out), (txt, txt_ref, txt_out)):
         for row in range(0, ROWS, QUARTER):
@@ -326,14 +334,17 @@
     group = 16 * rows
     n_img, n_txt = len(img_edges()), len(txt_edges())
     vmem = pl.BlockSpec(memory_space=pltpu.VMEM)
-    smem = pl.BlockSpec(memory_space=pltpu.SMEM)
+    hbm = pl.BlockSpec(memory_space=pltpu.HBM)
     return pl.pallas_call(
         kernel,
-        out_shape=[jax.ShapeDtypeStruct((rows, width), jnp.float32)] * 2,
-        in_specs=[vmem, vmem, smem, smem],
+        out_shape=[pltpu.VMEM((rows, width), jnp.float32)] * 2,
+        in_specs=[pl.BlockSpec(memory_space=pl.ANY)] * 4,
         out_specs=[vmem, vmem],
         scratch_shapes=(
-            [pltpu.VMEM((group, width), jnp.bfloat16)] * 2
+            [pltpu.VMEM((rows, width), jnp.bfloat16)] * 2
+            + [pltpu.VMEM((1,), jnp.float32)] * 2
+            + [pltpu.SemaphoreType.DMA((4,))]
+            + [pltpu.VMEM((group, width), jnp.bfloat16)] * 2
             + [pltpu.VMEM((group, group), jnp.bfloat16)]
             + [pltpu.VMEM((group, width), jnp.float32)] * 2
             + [pltpu.VMEM((group, width), jnp.bfloat16)] * 4

time: 60.4 us -> 53.8 us (0.89); the launches traced: 59.2 us -> 53.7 us
  Pallas kernels: 54.9 us -> 50.3 us
  local copies, waits for them, and re-layouts: 2.46 us -> 1.43 us
    pallas_call x1, Pallas kernels: 54.9 us -> 50.3 us  [on_device(): pl.pallas_call(kernel, out_shape=[pltpu.VMEM((rows, width), jnp.float32)]...]
    unnamed x4 -> x2, local copies, waits for them, and re-layouts: 2.46 us -> 1.43 us
where the time goes in v2:
time: 53.8 us; the launch traced here: 53.7 us
  Pallas kernels  50.3 us (93%)
  between operations  1.93 us (4%)
  local copies, waits for them, and re-layouts  1.43 us (3%)
    pallas_call x1, Pallas kernels, on_device(): pl.pallas_call(kernel, out_shape=[pltpu.VMEM((rows, width), jnp.float32)]...  50.3 us
    unnamed x2, local copies, waits for them, and re-layouts  1.43 us

profile of v2, /device:TPU:1, one launch (start us, length us, event | category | flops | bytes accessed | tf_op | source)
XLA Modules:
  0.0 53.7 jit_solution(8999227048064729227)
XLA Ops:
  1.9 50.3 %shard_map.59 = (f32[64,1152]{1,0:T(8,128)S(1)}, f32[64,1152]{1,0:T(8,128)S(1)}) custom-call(bf16[64,1152]{1,0:T(8,128)(2,1)} %img_hbm.1, bf16[64,1152]{1,0:T(8,128)(2,1)} %txt_hbm.1, f32[1]{0:T(128)S(6)} %copy.10.temp_hbm, f32[1]{0:T(128)S(6)} %copy.11.bias_hbm), custom_call_target="tpu_custom_call" | custom-call | tf_op jit(solution)/shard_map/pallas_call | solution.py:338
  52.3 0.7 %copy.8 = f32[64,1152]{1,0:T(8,128)} copy(f32[64,1152]{1,0:T(8,128)S(1)} %get-tuple-element.2) | data formatting | bytes 589824
  53.0 0.7 %copy.9 = f32[64,1152]{1,0:T(8,128)} copy(f32[64,1152]{1,0:T(8,128)S(1)} %get-tuple-element.3) | data formatting | bytes 589824

commit v3 on v2

--- a/solution.py
+++ b/solution.py
@@ -24,13 +24,89 @@
     + [((0, d), 0) for d in (1, 3)] + [((d, 0), 1) for d in (1, 3)]
     + [((2, 0), 0), ((0, 2), 1)]
     + [((3, d), 0) for d in (1, 3)] + [((d, 3), 1) for d in (1, 3)]
-    + [((0, 2), 0), ((2, 0), 1)]
     + [((1, d), 0) for d in (1, 3)] + [((d, 1), 1) for d in (1, 3)]
     + [((2, d), 0) for d in (1, 3)] + [((d, 2), 1) for d in (1, 3)]
+    + [((0, 2), 0), ((2, 0), 1)]
     + [((3, 2), 0), ((2, 3), 1), ((1, 2), 0), ((2, 1), 1), ((2, 2), 0), ((2, 2), 1)]
 )
 TXT_UNITS = [((dz, s), 0) for dz in (0, 1, 7, 2, 6, 3, 5, 4) for s in (0, 1)]
 
+
+PLAN = (
+    ("send", "t", "z", 0, 1, 0), ("send", "t", "z", 0, -1, 2), ("send", "i", "f", "A", 0, 1, 0),
+    ("send", "i", "f", "A", 0, -1, 0), ("send", "t", "z", 0, 1, 1), ("send", "i", "f", "B", 0, -1, 0),
+    ("send", "t", "z", 0, 1, 2), ("send", "i", "f", "B", 0, 1, 0), ("send", "i", "f", "A", 0, -1, 1),
+    ("send", "i", "f", "B", 0, 1, 1), ("send", "i", "s", "A", 0, -1, 0), ("send", "i", "s", "B", 0, 1, 1),
+    ("send", "t", "z", 0, 1, 3), ("send", "t", "z", 0, -1, 3), ("send", "i", "f", "A", 0, 1, 1),
+    ("send", "i", "s", "B", 0, -1, 0), ("send", "i", "s", "B", 0, -1, 1), ("send", "t", "z", 0, -1, 0),
+    ("send", "i", "s", "A", 0, 1, 0), ("send", "i", "s", "B", 0, 1, 0), ("send", "i", "s", "A", 0, -1, 1),
+    ("send", "t", "z", 0, -1, 1), ("send", "i", "f", "B", 0, -1, 1), ("send", "t", "c", 0, 1),
+    ("send", "i", "s", "A", 0, 1, 1), ("send", "t", "c", 0, 0), ("send", "t", "z", 1, 1, 0),
+    ("send", "t", "z", 1, -1, 2), ("send", "i", "fq", "A", 0, 1, 0), ("send", "i", "fq", "A", 0, -1, 0),
+    ("send", "i", "fq", "B", 0, -1, 0), ("send", "i", "fq", "B", 0, 1, 0), ("send", "t", "z", 1, 1, 1),
+    ("send", "t", "z", 1, -1, 3), ("send", "i", "s", "B", 1, 1, 1), ("send", "i", "s", "A", 3, -1, 1),
+    ("send", "i", "s", "B", 3, -1, 1), ("send", "t", "c", 1, 1), ("send", "i", "s", "A", 3, 1, 0),
+    ("send", "t", "z", 1, -1, 0), ("send", "i", "s", "B", 3, 1, 0), ("send", "i", "s", "B", 3, -1, 0),
+    ("send", "t", "z", 1, 1, 2), ("send", "i", "s", "A", 3, -1, 0), ("send", "i", "s", "A", 3, 1, 1),
+    ("send", "i", "s", "B", 3, 1, 1), ("send", "i", "sq", "B", 0, -1, 0), ("send", "t", "z", 1, -1, 1),
+    ("send", "t", "z", 1, 1, 3), ("send", "i", "s", "B", 1, -1, 0), ("send", "i", "s", "B", 1, 1, 0),
+    ("send", "i", "s", "A", 1, -1, 0), ("send", "i", "s", "A", 1, 1, 0), ("send", "i", "sq", "A", 0, -1, 0),
+    ("send", "i", "sq", "A", 0, 1, 0), ("send", "t", "z", 2, 1, 0), ("send", "t", "z", 2, -1, 2),
+    ("send", "t", "c", 1, 0), ("send", "i", "s", "A", 2, 1, 0), ("send", "i", "s", "A", 2, -1, 0),
+    ("send", "i", "s", "A", 1, 1, 1), ("send", "i", "s", "B", 2, -1, 0), ("send", "i", "s", "B", 2, 1, 0),
+    ("send", "t", "z", 2, 1, 1), ("send", "t", "z", 2, -1, 3), ("send", "i", "s", "A", 1, -1, 1),
+    ("send", "i", "s", "A", 2, -1, 1), ("send", "t", "c", 7, 0), ("send", "i", "s", "B", 1, -1, 1),
+    ("send", "i", "s", "B", 2, 1, 1), ("send", "t", "c", 2, 1), ("send", "t", "c", 6, 0),
+    ("send", "t", "z", 2, -1, 0), ("send", "i", "s", "A", 2, 1, 1), ("send", "i", "sq", "B", 3, -1, 0),
+    ("send", "i", "sq", "B", 3, 1, 0), ("send", "t", "c", 7, 1), ("send", "t", "z", 2, 1, 2),
+    ("send", "i", "s", "B", 2, -1, 1), ("send", "t", "z", 2, -1, 1), ("send", "i", "sq", "A", 3, 1, 0),
+    ("send", "i", "sq", "A", 3, -1, 0), ("send", "t", "z", 2, 1, 3), ("send", "i", "sq", "B", 0, 1, 0),
+    ("send", "t", "c", 2, 0), ("send", "i", "sq", "A", 1, -1, 0), ("send", "t", "c", 6, 1),
+    ("send", "t", "z", 3, 1, 0), ("send", "t", "z", 3, -1, 2), ("send", "i", "sq", "A", 1, 1, 0),
+    ("send", "i", "sq", "B", 1, 1, 0), ("send", "i", "sq", "B", 1, -1, 0), ("coef", 0, 384, 0, 384), ("own",),
+    ("send", "t", "z", 3, 1, 1), ("send", "t", "z", 3, -1, 3), ("send", "i", "sq", "A", 2, -1, 0),
+    ("send", "i", "sq", "B", 2, 1, 0), ("send", "t", "c", 5, 0), ("send", "i", "sq", "A", 2, 1, 0),
+    ("send", "i", "sq", "B", 2, -1, 0), ("send", "t", "c", 3, 1), ("coef", 384, 256, 0, 640),
+    ("coef", 0, 384, 384, 256), ("send", "t", "c", 3, 0), ("send", "t", "c", 5, 1), ("coef", 0, 640, 640, 256),
+    ("coef", 640, 256, 0, 896), ("send", "t", "c", 4, 0), ("send", "t", "c", 4, 1), ("coef", 0, 896, 896, 128),
+    ("coef", 896, 128, 0, 1024), ("txt", 896, 128, 0, 1024), ("give", "t", "c", 4, 1), ("give", "t", "c", 4, 0),
+    ("img", 896, 128, 0, 1024), ("give", "i", "sq", "A", 2, 1, 0), ("give", "i", "sq", "B", 2, -1, 0),
+    ("give", "i", "sq", "B", 2, 1, 0), ("give", "i", "sq", "A", 2, -1, 0), ("txt", 640, 256, 0, 1024),
+    ("give", "t", "z", 3, -1, 2), ("give", "t", "z", 3, 1, 0), ("give", "t", "z", 3, 1, 1),
+    ("give", "i", "sq", "A", 1, 1, 0), ("img", 768, 128, 0, 1024), ("give", "i", "sq", "A", 1, -1, 0),
+    ("give", "i", "sq", "B", 3, -1, 0), ("give", "i", "sq", "B", 1, 1, 0), ("give", "i", "sq", "B", 3, 1, 0),
+    ("give", "t", "c", 3, 0), ("give", "t", "c", 5, 1), ("give", "t", "c", 5, 0), ("give", "i", "sq", "A", 3, -1, 0),
+    ("give", "t", "z", 3, -1, 3), ("give", "i", "sq", "B", 1, -1, 0), ("give", "i", "sq", "B", 0, 1, 0),
+    ("give", "i", "sq", "A", 3, 1, 0), ("img", 512, 256, 0, 1024), ("give", "t", "z", 2, -1, 0),
+    ("give", "t", "z", 2, 1, 2), ("give", "i", "sq", "B", 0, -1, 0), ("give", "i", "s", "B", 2, -1, 1),
+    ("give", "t", "z", 2, 1, 3), ("give", "t", "c", 3, 1), ("give", "t", "z", 2, -1, 1),
+    ("give", "i", "s", "A", 2, 1, 1), ("give", "i", "sq", "A", 0, 1, 0), ("give", "i", "s", "B", 2, 1, 1),
+    ("give", "i", "s", "A", 2, -1, 1), ("txt", 384, 256, 0, 1024), ("give", "i", "s", "A", 2, 1, 0),
+    ("give", "i", "s", "A", 1, -1, 1), ("give", "i", "s", "B", 2, -1, 0), ("give", "t", "c", 2, 0),
+    ("give", "i", "s", "B", 2, 1, 0), ("give", "i", "s", "A", 1, 1, 1), ("give", "i", "s", "A", 2, -1, 0),
+    ("give", "i", "sq", "A", 0, -1, 0), ("give", "t", "z", 2, -1, 2), ("give", "t", "z", 2, 1, 0),
+    ("img", 256, 256, 0, 1024), ("give", "t", "z", 2, 1, 1), ("give", "t", "z", 2, -1, 3), ("give", "t", "c", 6, 1),
+    ("give", "i", "s", "A", 1, -1, 0), ("give", "i", "s", "A", 3, 1, 0), ("give", "i", "s", "B", 1, 1, 1),
+    ("give", "i", "s", "B", 1, 1, 0), ("give", "i", "s", "B", 1, -1, 1), ("give", "i", "s", "B", 3, -1, 0),
+    ("txt", 128, 256, 0, 1024), ("give", "t", "z", 1, 1, 2), ("give", "t", "z", 1, -1, 0), ("give", "t", "c", 6, 0),
+    ("give", "i", "s", "B", 3, 1, 1), ("give", "i", "s", "A", 3, -1, 0), ("give", "i", "s", "B", 1, -1, 0),
+    ("give", "i", "s", "B", 3, 1, 0), ("give", "i", "s", "A", 3, -1, 1), ("give", "i", "s", "A", 3, 1, 1),
+    ("give", "i", "s", "B", 3, -1, 1), ("give", "t", "c", 7, 0), ("give", "i", "s", "A", 1, 1, 0),
+    ("give", "t", "c", 7, 1), ("give", "t", "c", 2, 1), ("give", "t", "z", 1, 1, 3), ("give", "t", "z", 1, -1, 1),
+    ("img", 0, 256, 0, 1024), ("give", "t", "z", 1, 1, 0), ("give", "t", "z", 1, -1, 2),
+    ("give", "i", "fq", "B", 0, -1, 0), ("give", "i", "fq", "A", 0, -1, 0), ("give", "i", "fq", "A", 0, 1, 0),
+    ("give", "t", "c", 1, 1), ("give", "i", "fq", "B", 0, 1, 0), ("give", "i", "s", "B", 0, -1, 1),
+    ("give", "i", "s", "A", 0, -1, 1), ("give", "i", "s", "A", 0, 1, 1), ("give", "i", "s", "B", 0, 1, 0),
+    ("give", "t", "z", 1, 1, 1), ("give", "t", "z", 1, -1, 3), ("give", "i", "s", "B", 0, -1, 0),
+    ("give", "t", "c", 1, 0), ("give", "i", "s", "B", 0, 1, 1), ("txt", 0, 128, 0, 1024),
+    ("give", "i", "s", "A", 0, 1, 0), ("give", "t", "z", 0, 1, 2), ("give", "t", "z", 0, -1, 0),
+    ("give", "i", "f", "B", 0, -1, 1), ("give", "t", "z", 0, 1, 3), ("give", "t", "z", 0, -1, 1),
+    ("give", "t", "c", 0, 0), ("give", "t", "c", 0, 1), ("give", "i", "f", "A", 0, 1, 1),
+    ("give", "i", "f", "B", 0, 1, 1), ("give", "i", "f", "A", 0, -1, 1), ("give", "i", "s", "A", 0, -1, 0),
+    ("give", "t", "z", 0, 1, 0), ("give", "t", "z", 0, -1, 2), ("give", "i", "f", "B", 0, -1, 0),
+    ("give", "i", "f", "B", 0, 1, 0), ("give", "i", "f", "A", 0, 1, 0), ("give", "i", "f", "A", 0, -1, 0),
+    ("give", "t", "z", 0, 1, 1), ("give", "t", "z", 0, -1, 3),
+)
 
 class Edge:
     def __init__(self, src, dst, row, count, axis, sign):
@@ -47,12 +123,14 @@
             return (df % 4, ds % 4) if first == "x" else (ds % 4, df % 4)
 
         for sg in (1, -1):
-            quarter = base + (0 if sg == 1 else QUARTER)
-            edges[half, "f", sg] = Edge(at(0, 0), at(-sg, 0), base, HALF, first, sg)
-            edges[half, "fq", sg] = Edge(at(-sg, 0), at(2, 0), quarter, QUARTER, first, sg)
+            rows = (base, base + QUARTER) if sg == 1 else (base + QUARTER, base)
+            for i in (0, 1):
+                edges["f", half, 0, sg, i] = Edge(at(0, 0), at(-sg, 0), rows[i], QUARTER, first, sg)
+            edges["fq", half, 0, sg, 0] = Edge(at(-sg, 0), at(2, 0), rows[0], QUARTER, first, sg)
             for df in range(4):
-                edges[half, "s", df, sg] = Edge(at(df, 0), at(df, -sg), base, HALF, second, sg)
-                edges[half, "sq", df, sg] = Edge(at(df, -sg), at(df, 2), quarter, QUARTER, second, sg)
+                for i in (0, 1):
+                    edges["s", half, df, sg, i] = Edge(at(df, 0), at(df, -sg), rows[i], QUARTER, second, sg)
+                edges["sq", half, df, sg, 0] = Edge(at(df, -sg), at(df, 2), rows[0], QUARTER, second, sg)
     return edges
 
 
@@ -65,7 +143,8 @@
                     ((-sg * k) % NZ, 0), ((-sg * (k + 1)) % NZ, 0), c * QUARTER, QUARTER, "z", sg
                 )
     for dz in range(NZ):
-        edges["c", dz] = Edge((dz, 0), (dz, 1), 0, ROWS, "c", 1)
+        for h in (0, 1):
+            edges["c", dz, h] = Edge((dz, 0), (dz, 1), h * HALF, HALF, "c", 1)
     return edges
 
 
@@ -73,7 +152,7 @@
     def __init__(self, units, edges, rows, part, out, back, sems, place):
         self.unit = 16 * ROWS // len(units)
         self.at = {unit: i * self.unit for i, unit in enumerate(units)}
-        self.done = set()
+        self.done = {}
         self.edges = edges
         self.number = {key: i for i, key in enumerate(edges)}
         self.rows, self.part, self.out, self.back = rows, part, out, back
@@ -128,7 +207,7 @@
                 self.seen.add(key)
 
     def total(self, slot, row, count):
-        assert self.span(slot, row, count).start in self.done
+        assert self.done[self.span(slot, row, count).start] == 16 * ROWS
         value = self.part[self.span(slot, row, count), :]
         for key, e in self.edges.items():
             if e.src == slot and e.row <= row and row + count <= e.row + e.count:
@@ -138,6 +217,14 @@
                     self.taken.add(key)
                 value = value + self.back[self.span(e.dst, row, count), :].astype(jnp.float32)
         return value
+
+    def add(self, part, start, count, first, length):
+        had = {self.done.get(row, 0) for row in range(start, start + count, QUARTER)}
+        assert len(had) == 1
+        had = had.pop()
+        for row in range(start, start + count, QUARTER):
+            self.done[row] = had + length
+        return part if had == 0 else self.part[start:start + count, :] + part
 
     def give(self, *keys):
         for key in keys:
@@ -228,98 +315,31 @@
         same = lax.broadcasted_iota(jnp.int32, dots.shape, 0) == lax.broadcasted_iota(jnp.int32, dots.shape, 1)
         coef[0:ROWS, 0:128] = (half_tau * wave + jnp.where(same, -half_tau, half_tau)).astype(jnp.bfloat16)
 
-    def img_grads(i0, n):
-        img.done.update(range(i0, i0 + n, QUARTER))
-        p_part[i0:i0 + n, :] = lax.dot_general(coef[:, i0:i0 + n], q_rows[...], TN,
-                                               preferred_element_type=jnp.float32)
-
-    def txt_grads(t0, n):
-        txt.done.update(range(t0, t0 + n, QUARTER))
-        q_part[t0:t0 + n, :] = lax.dot_general(coef[t0:t0 + n, :], p_rows[...], NN,
-                                               preferred_element_type=jnp.float32)
-
-    both = (1, -1)
-
-    def ring(k, *places):
-        for i in places:
-            for sg in both:
-                txt.send(("z", k, sg, CHUNKS[sg][i]))
-
-    def ring_back(k, *places):
-        for i in places:
-            for sg in both:
-                txt.give(("z", k, sg, CHUNKS[sg][i]))
-
-    def across(kind, *far, way=img.send):
-        for df in far:
-            for half in "AB":
-                for sg in both:
-                    way((half, kind, df, sg))
-
-    def along(kind, way=img.send):
-        for half in "AB":
-            for sg in both:
-                way((half, kind, sg))
-
-    along("f")
-    ring(0, 0, 1, 2, 3)
-    across("s", 0)
-    txt.send(("c", 0))
-    ring(1, 0)
-    along("fq")
-    across("s", 3)
-    ring(1, 1, 2)
-    across("sq", 0)
-    ring(1, 3)
-    txt.send(("c", 1), ("c", 7))
-    across("s", 1)
-    ring(2, 0)
-    across("s", 2)
-    ring(2, 1)
-    scores(0, 384, 0, 384)
-    own_scores()
-    ring(2, 2)
-    across("sq", 3)
-    ring(2, 3)
-    txt.send(("c", 2), ("c", 6))
-    ring(3, 0)
-    scores(384, 256, 0, 384)
-    ring(3, 1)
-    across("sq", 1)
-    scores(0, 640, 384, 256)
-    txt.send(("c", 3), ("c", 5))
-    across("sq", 2)
-    txt.send(("c", 4))
-    scores(640, 256, 0, 640)
-    scores(0, 896, 640, 256)
-    scores(0, 896, 896, 128)
-    scores(896, 128, 0, 1024)
-
-    txt_grads(896, 128)
-    txt.give(("c", 4))
-    img_grads(768, 256)
-    across("sq", 2, 3, 1, way=img.give)
-    txt_grads(640, 256)
-    txt.give(("c", 3), ("c", 5))
-    ring_back(3, 0, 1)
-    img_grads(512, 256)
-    across("sq", 0, way=img.give)
-    ring_back(2, 2, 3)
-    across("s", 2, way=img.give)
-    txt_grads(384, 256)
-    txt.give(("c", 2), ("c", 6))
-    ring_back(2, 0, 1)
-    img_grads(256, 256)
-    across("s", 3, 1, way=img.give)
-    ring_back(1, 2, 3)
-    txt_grads(0, 384)
-    txt.give(("c", 1), ("c", 7), ("c", 0))
-    ring_back(1, 0, 1)
-    img_grads(0, 256)
-    along("fq", way=img.give)
-    across("s", 0, way=img.give)
-    ring_back(0, 2, 3, 0, 1)
-    along("f", way=img.give)
+    def img_grads(i0, n, t0, tn):
+        part = lax.dot_general(coef[t0:t0 + tn, i0:i0 + n], q_rows[t0:t0 + tn, :], TN,
+                               preferred_element_type=jnp.float32)
+        p_part[i0:i0 + n, :] = img.add(part, i0, n, t0, tn)
+
+    def txt_grads(t0, n, i0, tn):
+        part = lax.dot_general(coef[t0:t0 + n, i0:i0 + tn], p_rows[i0:i0 + tn, :], NN,
+                               preferred_element_type=jnp.float32)
+        q_part[t0:t0 + n, :] = txt.add(part, t0, n, i0, tn)
+
+    sides = {"i": img, "t": txt}
+    for step in PLAN:
+        if step[0] == "send":
+            sides[step[1]].send(step[2:])
+        elif step[0] == "give":
+            sides[step[1]].give(step[2:])
+        elif step[0] == "coef":
+            scores(*step[1:])
+        elif step[0] == "own":
+            assert ("coef", 0, 384, 0, 384) in PLAN[: PLAN.index(step)]
+            own_scores()
+        elif step[0] == "img":
+            img_grads(*step[1:])
+        else:
+            txt_grads(*step[1:])
 
     for side, ref, out in ((img, img_ref, img_out), (txt, txt_ref, txt_out)):
         for row in range(0, ROWS, QUARTER):
@@ -329,13 +349,24 @@
     txt.finish()
 
 
+def store_kernel(img_ref, txt_ref, img_out, txt_out, sems):
+    stores = [
+        pltpu.make_async_copy(here, there, sems.at[i])
+        for i, (here, there) in enumerate(((img_ref, img_out), (txt_ref, txt_out)))
+    ]
+    for store in stores:
+        store.start()
+    for store in stores:
+        store.wait()
+
+
 def on_device(image_emb, text_emb, log_temp, bias):
     rows, width = image_emb.shape
     group = 16 * rows
     n_img, n_txt = len(img_edges()), len(txt_edges())
     vmem = pl.BlockSpec(memory_space=pltpu.VMEM)
     hbm = pl.BlockSpec(memory_space=pltpu.HBM)
-    return pl.pallas_call(
+    grads = pl.pallas_call(
         kernel,
         out_shape=[pltpu.VMEM((rows, width), jnp.float32)] * 2,
         in_specs=[pl.BlockSpec(memory_space=pl.ANY)] * 4,
@@ -355,6 +386,14 @@
             collective_id=0, has_side_effects=True, vmem_limit_bytes=56 * 2**20
         ),
     )(image_emb, text_emb, log_temp, bias)
+    anywhere = pl.BlockSpec(memory_space=pl.ANY)
+    return pl.pallas_call(
+        store_kernel,
+        out_shape=[jax.ShapeDtypeStruct((rows, width), jnp.float32)] * 2,
+        in_specs=[vmem] * 2,
+        out_specs=[anywhere] * 2,
+        scratch_shapes=[pltpu.SemaphoreType.DMA((2,))],
+    )(*(pltpu.with_memory_space_constraint(grad, pltpu.VMEM) for grad in grads))
 
 
 def solution(mesh):

time: 53.8 us -> 51.3 us (0.954)
  local copies, waits for them, and re-layouts: 1.43 us -> 0 us
  Pallas kernels: 50.3 us -> 49.3 us
    pallas_call x1, Pallas kernels: 50.3 us -> 48.4 us  [on_device(): pl.pallas_call(kernel, out_shape=[pltpu.VMEM((rows, width), jnp.float32)]...]
    unnamed x2 -> x0, local copies, waits for them, and re-layouts: 1.43 us -> none
    pallas_call x0 -> x1, Pallas kernels: none -> 0.83 us  [on_device(): pl.pallas_call(store_kernel, out_shape=[jax.ShapeDtypeStruct((rows, width...]
where the time goes in v3:
time: 51.3 us; the launch traced here: 51.2 us
  Pallas kernels  49.3 us (96%)
  between operations  1.93 us (4%)
    pallas_call x1, Pallas kernels, on_device(): pl.pallas_call(kernel, out_shape=[pltpu.VMEM((rows, width), jnp.float32)]...  48.4 us

profile of v3, /device:TPU:1, one launch (start us, length us, event | category | flops | bytes accessed | tf_op | source)
XLA Modules:
  0.0 51.2 jit_solution(14899623568343132486)
XLA Ops:
  1.9 48.4 %shard_map.59 = (f32[64,1152]{1,0:T(8,128)S(1)}, f32[64,1152]{1,0:T(8,128)S(1)}) custom-call(bf16[64,1152]{1,0:T(8,128)(2,1)} %img_hbm.1, bf16[64,1152]{1,0:T(8,128)(2,1)} %txt_hbm.1, f32[1]{0:T(128)S(6)} %copy.6.temp_hbm, f32[1]{0:T(128)S(6)} %copy.7.bias_hbm), custom_call_target="tpu_custom_call" | custom-call | tf_op jit(solution)/shard_map/pallas_call | solution.py:369
  50.4 0.8 %shard_map.60 = (f32[64,1152]{1,0:T(8,128)}, f32[64,1152]{1,0:T(8,128)}) custom-call(f32[64,1152]{1,0:T(8,128)S(1)} %get-tuple-element.4.img_ref, f32[64,1152]{1,0:T(8,128)S(1)} %get-tuple-element.5.txt_ref), custom_call_target="tpu_custom_call" | custom-call | tf_op jit(solution)/shard_map/pallas_call | solution.py:390

commit v4 on v3

v4 whole, which is shorter than its diff:
```python
import functools

import jax
import jax.numpy as jnp
from jax import lax
from jax.experimental import pallas as pl
from jax.experimental.pallas import tpu as pltpu
from jax.sharding import PartitionSpec as P

EPS = 1e-06
MESH = pl.DeviceIdType.MESH
NX, NY, NZ = 4, 4, 8
ROWS = 64
HALF = ROWS // 2
QUARTER = ROWS // 4
NT = (((1,), (1,)), ((), ()))
TN = (((0,), (0,)), ((), ()))
NN = (((1,), (0,)), ((), ()))
CHUNKS = {1: (0, 1, 2, 3), -1: (2, 3, 0, 1)}

IMG_UNITS = (
    [((0, 0), 0), ((0, 0), 1)]
    + [((d, 0), 0) for d in (1, 3)] + [((0, d), 1) for d in (1, 3)]
    + [((0, d), 0) for d in (1, 3)] + [((d, 0), 1) for d in (1, 3)]
    + [((2, 0), 0), ((0, 2), 1)]
    + [((3, d), 0) for d in (1, 3)] + [((d, 3), 1) for d in (1, 3)]
    + [((1, d), 0) for d in (1, 3)] + [((d, 1), 1) for d in (1, 3)]
    + [((2, d), 0) for d in (1, 3)] + [((d, 2), 1) for d in (1, 3)]
    + [((0, 2), 0), ((2, 0), 1)]
    + [((3, 2), 0), ((2, 3), 1), ((1, 2), 0), ((2, 1), 1), ((2, 2), 0), ((2, 2), 1)]
)
TXT_UNITS = [((dz, s), 0) for dz in (0, 1, 7, 2, 6, 3, 5, 4) for s in (0, 1)]


PLAN = (
    ("send", "t", "z", 0, -1, 2), ("send", "t", "z", 0, 1, 0), ("send", "t", "z", 0, -1, 3),
    ("send", "i", "f", "A", 0, 1, 0), ("send", "i", "f", "B", 0, -1, 0), ("send", "t", "z", 0, 1, 1),
    ("send", "i", "f", "B", 0, 1, 0), ("send", "i", "f", "A", 0, -1, 0), ("send", "t", "z", 0, -1, 0),
    ("send", "i", "f", "A", 0, 1, 1), ("send", "t", "z", 0, 1, 3), ("send", "i", "s", "A", 0, -1, 0),
    ("send", "i", "s", "B", 0, -1, 1), ("send", "t", "z", 0, 1, 2), ("send", "i", "f", "B", 0, -1, 1),
    ("send", "i", "s", "B", 0, 1, 0), ("send", "i", "s", "A", 0, 1, 1), ("send", "i", "f", "B", 0, 1, 1),
    ("send", "i", "s", "A", 0, 1, 0), ("send", "i", "s", "B", 0, 1, 1), ("send", "i", "f", "A", 0, -1, 1),
    ("send", "i", "s", "B", 0, -1, 0), ("send", "i", "s", "A", 0, -1, 1), ("send", "t", "z", 0, -1, 1),
    ("send", "t", "z", 1, -1, 2), ("send", "t", "z", 1, 1, 0), ("send", "i", "fq", "A", 0, 1, 0),
    ("send", "i", "fq", "B", 0, -1, 0), ("send", "i", "s", "A", 1, -1, 0), ("send", "i", "fq", "A", 0, -1, 0),
    ("send", "i", "fq", "B", 0, 1, 0), ("send", "i", "s", "B", 1, 1, 1), ("send", "i", "s", "B", 3, -1, 1),
    ("send", "t", "z", 1, -1, 3), ("send", "t", "z", 1, 1, 1), ("send", "i", "s", "B", 3, 1, 0),
    ("send", "i", "sq", "A", 0, -1, 0), ("send", "i", "s", "B", 1, -1, 0), ("send", "i", "s", "A", 3, 1, 0),
    ("send", "t", "z", 1, -1, 0), ("send", "i", "sq", "B", 0, 1, 0), ("send", "t", "c", 1, 1),
    ("send", "t", "z", 1, 1, 3), ("send", "t", "c", 7, 0), ("send", "i", "s", "B", 3, -1, 0),
    ("send", "i", "s", "B", 3, 1, 1), ("send", "i", "s", "A", 1, 1, 1), ("send", "i", "s", "A", 1, 1, 0),
    ("send", "i", "s", "A", 3, -1, 0), ("send", "i", "s", "B", 1, -1, 1), ("send", "t", "z", 1, -1, 1),
    ("send", "i", "s", "A", 1, -1, 1), ("send", "t", "z", 1, 1, 2), ("send", "i", "s", "A", 3, -1, 1),
    ("send", "t", "c", 7, 1), ("send", "t", "z", 2, -1, 2), ("send", "t", "z", 2, 1, 0),
    ("send", "i", "s", "A", 2, 1, 0), ("send", "i", "s", "B", 2, 1, 0), ("send", "t", "c", 0, 0),
    ("send", "i", "s", "A", 3, 1, 1), ("send", "t", "z", 2, -1, 3), ("send", "t", "z", 2, 1, 1),
    ("send", "t", "c", 0, 1), ("send", "t", "c", 2, 1), ("send", "i", "s", "B", 2, -1, 0),
    ("send", "i", "s", "A", 2, -1, 0), ("send", "t", "c", 6, 0), ("send", "i", "sq", "A", 3, 1, 0),
    ("send", "t", "c", 1, 0), ("send", "i", "s", "B", 1, 1, 0), ("send", "t", "z", 2, -1, 0),
    ("send", "i", "s", "B", 2, -1, 1), ("send", "i", "sq", "B", 3, 1, 0), ("send", "t", "z", 2, 1, 3),
    ("send", "i", "sq", "B", 0, -1, 0), ("send", "i", "s", "A", 2, -1, 1), ("send", "t", "z", 2, -1, 1),
    ("send", "i", "sq", "A", 3, -1, 0), ("send", "i", "s", "B", 2, 1, 1), ("send", "i", "sq", "A", 0, 1, 0),
    ("send", "t", "z", 2, 1, 2), ("coef", 0, 384, 0, 384), ("send", "i", "sq", "B", 3, -1, 0),
    ("send", "i", "sq", "A", 1, -1, 0), ("send", "i", "s", "A", 2, 1, 1), ("send", "i", "sq", "B", 1, -1, 0),
    ("send", "i", "sq", "A", 1, 1, 0), ("send", "t", "c", 2, 0), ("send", "t", "z", 3, -1, 2),
    ("send", "t", "z", 3, 1, 0), ("send", "i", "sq", "B", 2, 1, 0), ("send", "i", "sq", "A", 2, 1, 0),
    ("send", "t", "z", 3, -1, 3), ("send", "t", "z", 3, 1, 1), ("send", "t", "c", 5, 0), ("send", "t", "c", 6, 1),
    ("send", "t", "c", 3, 1), ("send", "i", "sq", "B", 1, 1, 0), ("send", "i", "sq", "B", 2, -1, 0),
    ("send", "i", "sq", "A", 2, -1, 0), ("coef", 0, 384, 384, 256), ("send", "t", "c", 3, 0),
    ("send", "t", "c", 5, 1), ("coef", 384, 256, 0, 640), ("own",), ("coef", 640, 256, 0, 896),
    ("send", "t", "c", 4, 1), ("send", "t", "c", 4, 0), ("coef", 0, 640, 640, 256), ("coef", 0, 896, 896, 128),
    ("coef", 896, 128, 0, 1024), ("txt", 896, 128), ("give", "t", "c", 4, 0), ("give", "t", "c", 4, 1),
    ("img", 896, 128), ("give", "i", "sq", "A", 2, -1, 0), ("give", "i", "sq", "B", 2, -1, 0),
    ("give", "i", "sq", "A", 2, 1, 0), ("give", "i", "sq", "B", 2, 1, 0), ("give", "i", "sq", "A", 1, 1, 0),
    ("img", 768, 128), ("give", "i", "sq", "B", 1, 1, 0), ("give", "i", "sq", "B", 1, -1, 0),
    ("give", "t", "z", 3, 1, 0), ("give", "i", "sq", "A", 1, -1, 0), ("give", "t", "z", 3, -1, 2), ("txt", 640, 256),
    ("give", "t", "c", 5, 1), ("give", "t", "z", 3, -1, 3), ("give", "t", "z", 3, 1, 1), ("give", "t", "c", 3, 0),
    ("give", "i", "sq", "B", 3, 1, 0), ("give", "i", "sq", "A", 3, 1, 0), ("give", "i", "sq", "A", 3, -1, 0),
    ("give", "i", "sq", "B", 3, -1, 0), ("img", 512, 256), ("give", "t", "z", 2, 1, 2), ("give", "t", "z", 2, -1, 0),
    ("give", "i", "s", "A", 2, 1, 1), ("give", "t", "z", 2, -1, 1), ("give", "t", "c", 3, 1),
    ("give", "i", "s", "B", 2, 1, 1), ("give", "t", "z", 2, 1, 3), ("give", "t", "c", 5, 0),
    ("give", "i", "s", "A", 2, -1, 1), ("give", "i", "s", "B", 2, -1, 1), ("txt", 384, 256),
    ("give", "i", "s", "A", 2, -1, 0), ("give", "i", "s", "A", 2, 1, 0), ("give", "i", "s", "B", 2, -1, 0),
    ("give", "i", "s", "B", 2, 1, 0), ("give", "i", "sq", "B", 0, 1, 0), ("give", "i", "sq", "A", 0, 1, 0),
    ("give", "t", "c", 2, 0), ("give", "i", "s", "A", 1, -1, 1), ("give", "i", "sq", "B", 0, -1, 0),
    ("give", "t", "z", 2, 1, 0), ("give", "i", "sq", "A", 0, -1, 0), ("give", "t", "z", 2, -1, 2), ("img", 256, 256),
    ("give", "t", "z", 2, -1, 3), ("give", "t", "z", 2, 1, 1), ("give", "i", "s", "A", 1, 1, 0),
    ("give", "i", "s", "B", 3, 1, 1), ("give", "i", "s", "B", 1, -1, 1), ("give", "t", "c", 6, 1),
    ("give", "i", "s", "B", 3, 1, 0), ("txt", 128, 256), ("give", "i", "s", "A", 3, -1, 1),
    ("give", "i", "s", "A", 1, 1, 1), ("give", "i", "s", "B", 3, -1, 1), ("give", "t", "c", 6, 0),
    ("give", "i", "s", "B", 1, 1, 0), ("give", "t", "z", 1, -1, 0), ("give", "t", "z", 1, 1, 2),
    ("give", "i", "s", "A", 1, -1, 0), ("give", "i", "s", "A", 3, 1, 0), ("give", "i", "s", "A", 3, 1, 1),
    ("give", "i", "s", "A", 3, -1, 0), ("give", "i", "s", "B", 3, -1, 0), ("give", "t", "c", 2, 1),
    ("give", "i", "s", "B", 1, 1, 1), ("give", "i", "s", "B", 1, -1, 0), ("give", "t", "z", 1, 1, 3),
    ("give", "t", "z", 1, -1, 1), ("img", 0, 256), ("give", "t", "z", 1, -1, 2), ("give", "t", "z", 1, 1, 0),
    ("give", "i", "fq", "B", 0, -1, 0), ("give", "t", "c", 1, 0), ("give", "i", "fq", "A", 0, -1, 0),
    ("give", "i", "fq", "A", 0, 1, 0), ("give", "i", "fq", "B", 0, 1, 0), ("give", "i", "s", "A", 0, 1, 1),
    ("give", "i", "s", "B", 0, 1, 1), ("give", "t", "c", 7, 0), ("give", "t", "c", 1, 1), ("give", "t", "c", 7, 1),
    ("give", "t", "z", 1, -1, 3), ("give", "t", "z", 1, 1, 1), ("give", "i", "s", "B", 0, 1, 0), ("txt", 0, 128),
    ("give", "i", "s", "A", 0, -1, 0), ("give", "i", "s", "A", 0, 1, 0), ("give", "i", "f", "A", 0, -1, 1),
    ("give", "i", "s", "B", 0, -1, 1), ("give", "t", "z", 0, -1, 0), ("give", "t", "z", 0, 1, 2),
    ("give", "t", "c", 0, 0), ("give", "i", "s", "A", 0, -1, 1), ("give", "t", "z", 0, -1, 1),
    ("give", "t", "z", 0, 1, 3), ("give", "t", "c", 0, 1), ("give", "i", "f", "B", 0, -1, 1),
    ("give", "i", "f", "A", 0, 1, 1), ("give", "i", "f", "B", 0, 1, 1), ("give", "i", "s", "B", 0, -1, 0),
    ("give", "t", "z", 0, -1, 2), ("give", "t", "z", 0, 1, 0), ("give", "i", "f", "B", 0, -1, 0),
    ("give", "i", "f", "B", 0, 1, 0), ("give", "i", "f", "A", 0, -1, 0), ("give", "i", "f", "A", 0, 1, 0),
    ("give", "t", "z", 0, -1, 3), ("give", "t", "z", 0, 1, 1),
)

class Edge:
    def __init__(self, src, dst, row, count, axis, sign):
        self.src, self.dst, self.row, self.count = src, dst, row, count
        self.axis, self.sign = axis, sign


def img_edges():
    edges = {}
    for half, first, second in (("A", "x", "y"), ("B", "y", "x")):
        base = 0 if half == "A" else HALF

        def at(df, ds, first=first):
            return (df % 4, ds % 4) if first == "x" else (ds % 4, df % 4)

        for sg in (1, -1):
            rows = (base, base + QUARTER) if sg == 1 else (base + QUARTER, base)
            for i in (0, 1):
                edges["f", half, 0, sg, i] = Edge(at(0, 0), at(-sg, 0), rows[i], QUARTER, first, sg)
            edges["fq", half, 0, sg, 0] = Edge(at(-sg, 0), at(2, 0), rows[0], QUARTER, first, sg)
            for df in range(4):
                for i in (0, 1):
                    edges["s", half, df, sg, i] = Edge(at(df, 0), at(df, -sg), rows[i], QUARTER, second, sg)
                edges["sq", half, df, sg, 0] = Edge(at(df, -sg), at(df, 2), rows[0], QUARTER, second, sg)
    return edges


def txt_edges():
    edges = {}
    for sg in (1, -1):
        for k in range(4):
            for c in CHUNKS[sg][: 4 if k < 3 else 2]:
                edges["z", k, sg, c] = Edge(
                    ((-sg * k) % NZ, 0), ((-sg * (k + 1)) % NZ, 0), c * QUARTER, QUARTER, "z", sg
                )
    for dz in range(NZ):
        for h in (0, 1):
            edges["c", dz, h] = Edge((dz, 0), (dz, 1), h * HALF, HALF, "c", 1)
    return edges


class Side:
    def __init__(self, units, edges, rows, part, out, back, sems, place):
        self.unit = 16 * ROWS // len(units)
        self.at = {unit: i * self.unit for i, unit in enumerate(units)}
        self.done = set()
        self.edges = edges
        self.number = {key: i for i, key in enumerate(edges)}
        self.rows, self.part, self.out, self.back = rows, part, out, back
        self.g_send, self.g_recv, self.r_send, self.r_recv = sems
        self.place = place
        self.sent, self.returned = set(), set()
        self.seen, self.taken = set(), set()

    def span(self, slot, row, count):
        return pl.ds(self.at[slot, row // self.unit] + row % self.unit, count)

    def gather_copy(self, key):
        e, i = self.edges[key], self.number[key]
        return pltpu.make_async_remote_copy(
            src_ref=self.rows.at[self.span(e.src, e.row, e.count)],
            dst_ref=self.rows.at[self.span(e.dst, e.row, e.count)],
            send_sem=self.g_send.at[i],
            recv_sem=self.g_recv.at[i],
            device_id=self.place(e.axis, e.sign),
            device_id_type=MESH,
        )

    def scatter_copy(self, key):
        e, i = self.edges[key], self.number[key]
        where = self.span(e.dst, e.row, e.count)
        return pltpu.make_async_remote_copy(
            src_ref=self.out.at[where],
            dst_ref=self.back.at[where],
            send_sem=self.r_send.at[i],
            recv_sem=self.r_recv.at[i],
            device_id=self.place(e.axis, -e.sign),
            device_id_type=MESH,
        )

    def send(self, *keys):
        for key in keys:
            e = self.edges[key]
            self.arrive(e.src, e.row, e.count)
            self.gather_copy(key).start()
            self.sent.add(key)

    def arrive_until(self, end):
        for (slot, which), start in self.at.items():
            if start < end:
                self.arrive(slot, which * self.unit, self.unit)

    def arrive(self, slot, row=0, count=ROWS):
        for key, e in self.edges.items():
            if e.dst == slot and e.row < row + count and row < e.row + e.count and key not in self.seen:
                assert key in self.sent, key
                self.gather_copy(key).wait_recv()
                self.seen.add(key)

    def total(self, slot, row, count):
        assert self.span(slot, row, count).start in self.done
        value = self.part[self.span(slot, row, count), :]
        for key, e in self.edges.items():
            if e.src == slot and e.row <= row and row + count <= e.row + e.count:
                if key not in self.taken:
                    assert key in self.returned, key
                    self.scatter_copy(key).wait_recv()
                    self.taken.add(key)
                value = value + self.back[self.span(e.dst, row, count), :].astype(jnp.float32)
        return value

    def passed(self, slot, row):
        return any(e.src == slot and e.row <= row < e.row + e.count for e in self.edges.values())

    def store(self, value, start):
        for (slot, which), first in self.at.items():
            if not start <= first < start + value.shape[0]:
                continue
            for row in range(0, self.unit, QUARTER):
                at = first + row
                rows = value[at - start:at - start + QUARTER, :]
                if self.passed(slot, which * self.unit + row):
                    self.part[at:at + QUARTER, :] = rows
                else:
                    self.out[at:at + QUARTER, :] = rows.astype(jnp.bfloat16)
                self.done.add(at)

    def give(self, *keys):
        for key in keys:
            e = self.edges[key]
            for row in range(e.row, e.row + e.count, QUARTER):
                where = self.span(e.dst, row, QUARTER)
                assert where.start in self.done
                if self.passed(e.dst, row):
                    self.out[where, :] = self.total(e.dst, row, QUARTER).astype(jnp.bfloat16)
            self.scatter_copy(key).start()
            self.returned.add(key)

    def take(self, last):
        own = {
            key: e for key, e in self.edges.items() if e.src == (0, 0) and (key[0] in ("f", "z")) == last
        }
        for key in own:
            assert key in self.returned
            self.scatter_copy(key).wait_recv()
            self.taken.add(key)
        for row in range(0, ROWS, QUARTER):
            value = self.part[self.span((0, 0), row, QUARTER), :]
            for e in own.values():
                if e.row <= row and row + QUARTER <= e.row + e.count:
                    value = value + self.back[self.span(e.dst, row, QUARTER), :].astype(jnp.float32)
            self.part[self.span((0, 0), row, QUARTER), :] = value

    def settle(self):
        for key in self.edges:
            self.gather_copy(key).wait_send()
            if self.edges[key].src != (0, 0):
                self.scatter_copy(key).wait_send()

    def finish(self):
        assert len(self.sent) == len(self.returned) == len(self.seen) == len(self.taken) == len(self.edges)
        for key in self.edges:
            if self.edges[key].src == (0, 0):
                self.scatter_copy(key).wait_send()


def unit_of(emb):
    wide = emb.astype(jnp.float32)
    inverse = lax.rsqrt(jnp.sum(wide * wide, axis=1, keepdims=True) + EPS)
    return wide * inverse, inverse


def back_norm(unit, inverse, grad):
    return inverse * (grad - unit * jnp.sum(unit * grad, axis=1, keepdims=True))


def kernel(
    img_hbm, txt_hbm, temp_hbm, bias_hbm, img_out, txt_out,
    img_ref, txt_ref, temp_ref, bias_ref, in_sems, img_unit, txt_unit, img_inv, txt_inv,
    p_rows, q_rows, coef, p_part, q_part, p_send, q_send, p_back, q_back,
    pg_send, pg_recv, pr_send, pr_recv, qg_send, qg_recv, qr_send, qr_recv,
):
    loads = [
        pltpu.make_async_copy(here, there, in_sems.at[i])
        for i, (here, there) in enumerate(
            ((img_hbm, img_ref), (txt_hbm, txt_ref), (temp_hbm, temp_ref), (bias_hbm, bias_ref))
        )
    ]
    for load in loads:
        load.start()
    dp, mp = lax.axis_index("dp"), lax.axis_index("mp")
    core, z, x = dp % 2, (dp // 2) % NZ, (dp // (2 * NZ)) * 2 + mp // NY
    y = mp % NY

    @functools.cache
    def place(axis, sign):
        nx, ny, nz, nc = x, y, z, core
        if axis == "x":
            nx = (x + sign + NX) % NX
        elif axis == "y":
            ny = (y + sign + NY) % NY
        elif axis == "z":
            nz = (z + sign + NZ) % NZ
        else:
            nc = 1 - core
        return ((nx // 2) * (2 * NZ) + nz * 2 + nc, (nx % 2) * NY + ny)

    barrier = pltpu.get_barrier_semaphore()
    neighbours = [place(a, s) for a in "xyz" for s in (1, -1)] + [place("c", 1)]
    for device in neighbours:
        pl.semaphore_signal(barrier, inc=1, device_id=device, device_id_type=MESH)

    img = Side(IMG_UNITS, img_edges(), p_rows, p_part, p_send, p_back,
               (pg_send, pg_recv, pr_send, pr_recv), place)
    txt = Side(TXT_UNITS, txt_edges(), q_rows, q_part, q_send, q_back,
               (qg_send, qg_recv, qr_send, qr_recv), place)

    loads[0].wait()
    unit, inverse = unit_of(img_ref[...])
    p_rows[0:ROWS, :] = unit.astype(jnp.bfloat16)
    img_unit[...] = unit
    img_inv[...] = jnp.broadcast_to(inverse, img_inv.shape)
    pl.semaphore_wait(barrier, len(neighbours))
    for sg in (1, -1):
        for half in "AB":
            img.send(("f", half, 0, sg, 0))
    for load in loads[1:]:
        load.wait()
    half_tau = 0.5 * jnp.exp(temp_ref[...].reshape(1, 1))
    half_bias = 0.5 * bias_ref[...].reshape(1, 1)

    unit, inverse = unit_of(txt_ref[...])
    q_rows[0:ROWS, :] = unit.astype(jnp.bfloat16)
    txt_unit[...] = unit
    txt_inv[...] = jnp.broadcast_to(inverse, txt_inv.shape)

    def scores(t0, tn, i0, n):
        txt.arrive_until(t0 + tn)
        img.arrive_until(i0 + n)
        dots = lax.dot_general(q_rows[t0:t0 + tn, :], p_rows[i0:i0 + n, :], NT,
                               preferred_element_type=jnp.float32)
        wave = jnp.tanh(half_tau * dots + half_bias)
        coef[t0:t0 + tn, i0:i0 + n] = (half_tau * wave + half_tau).astype(jnp.bfloat16)

    def own_scores():
        dots = lax.dot_general(q_rows[0:ROWS, :], p_rows[0:128, :], NT,
                               preferred_element_type=jnp.float32)
        wave = jnp.tanh(half_tau * dots + half_bias)
        same = lax.broadcasted_iota(jnp.int32, dots.shape, 0) == lax.broadcasted_iota(jnp.int32, dots.shape, 1)
        coef[0:ROWS, 0:128] = (half_tau * wave + jnp.where(same, -half_tau, half_tau)).astype(jnp.bfloat16)

    def img_grads(i0, n):
        img.store(lax.dot_general(coef[:, i0:i0 + n], q_rows[...], TN, preferred_element_type=jnp.float32), i0)

    def txt_grads(t0, n):
        txt.store(lax.dot_general(coef[t0:t0 + n, :], p_rows[...], NN, preferred_element_type=jnp.float32), t0)

    sides = {"i": img, "t": txt}
    for step in PLAN:
        if step[0] == "send" and (step[1] != "i" or step[2:] not in img.sent):
            sides[step[1]].send(step[2:])
        elif step[0] == "send":
            pass
        elif step[0] == "give":
            sides[step[1]].give(step[2:])
        elif step[0] == "coef":
            scores(*step[1:])
        elif step[0] == "own":
            assert ("coef", 0, 384, 0, 384) in PLAN[: PLAN.index(step)]
            own_scores()
        elif step[0] == "img":
            img_grads(*step[1:])
        else:
            txt_grads(*step[1:])

    for side in (img, txt):
        side.settle()
        side.take(last=False)
    for side, unit, inverse, out in ((img, img_unit, img_inv, img_out), (txt, txt_unit, txt_inv, txt_out)):
        side.take(last=True)
        out[...] = back_norm(unit[...], inverse[:, 0:1], side.part[0:ROWS, :])
    img.finish()
    txt.finish()


def store_kernel(img_ref, txt_ref, img_out, txt_out, sems):
    stores = [
        pltpu.make_async_copy(here, there, sems.at[i])
        for i, (here, there) in enumerate(((img_ref, img_out), (txt_ref, txt_out)))
    ]
    for store in stores:
        store.start()
    for store in stores:
        store.wait()


def on_device(image_emb, text_emb, log_temp, bias):
    rows, width = image_emb.shape
    group = 16 * rows
    n_img, n_txt = len(img_edges()), len(txt_edges())
    vmem = pl.BlockSpec(memory_space=pltpu.VMEM)
    hbm = pl.BlockSpec(memory_space=pltpu.HBM)
    grads = pl.pallas_call(
        kernel,
        out_shape=[pltpu.VMEM((rows, width), jnp.float32)] * 2,
        in_specs=[pl.BlockSpec(memory_space=pl.ANY)] * 4,
        out_specs=[vmem, vmem],
        scratch_shapes=(
            [pltpu.VMEM((rows, width), jnp.bfloat16)] * 2
            + [pltpu.VMEM((1,), jnp.float32)] * 2
            + [pltpu.SemaphoreType.DMA((4,))]
            + [pltpu.VMEM((rows, width), jnp.float32)] * 2
            + [pltpu.VMEM((rows, 128), jnp.float32)] * 2
            + [pltpu.VMEM((group, width), jnp.bfloat16)] * 2
            + [pltpu.VMEM((group, group), jnp.bfloat16)]
            + [pltpu.VMEM((group, width), jnp.float32)] * 2
            + [pltpu.VMEM((group, width), jnp.bfloat16)] * 4
            + [pltpu.SemaphoreType.DMA((n_img,))] * 4
            + [pltpu.SemaphoreType.DMA((n_txt,))] * 4
        ),
        compiler_params=pltpu.CompilerParams(
            collective_id=0, has_side_effects=True, vmem_limit_bytes=56 * 2**20
        ),
    )(image_emb, text_emb, log_temp, bias)
    anywhere = pl.BlockSpec(memory_space=pl.ANY)
    return pl.pallas_call(
        store_kernel,
        out_shape=[jax.ShapeDtypeStruct((rows, width), jnp.float32)] * 2,
        in_specs=[vmem] * 2,
        out_specs=[anywhere] * 2,
        scratch_shapes=[pltpu.SemaphoreType.DMA((2,))],
    )(*(pltpu.with_memory_space_constraint(grad, pltpu.VMEM) for grad in grads))


def solution(mesh):
    placed = (P(("dp", "mp"), None), P(("dp", "mp"), None), P(), P())
    return jax.shard_map(
        on_device,
        mesh=mesh,
        in_specs=placed,
        out_specs=(P(("dp", "mp"), None), P(("dp", "mp"), None)),
        check_vma=False,
    )
```

time: 51.3 us -> 50.7 us (0.988)
  Pallas kernels: 49.3 us -> 48.6 us
    pallas_call x1, Pallas kernels: 48.4 us -> 47.8 us  [on_device(): pl.pallas_call(kernel, out_shape=[pltpu.VMEM((rows, width), jnp.float32)]...]
where the time goes in v4:
time: 50.7 us; the launch traced here: 50.6 us
  Pallas kernels  48.6 us (96%)
  between operations  1.93 us (4%)
    pallas_call x1, Pallas kernels, on_device(): pl.pallas_call(kernel, out_shape=[pltpu.VMEM((rows, width), jnp.float32)]...  47.8 us

profile of v4, /device:TPU:1, one launch (start us, length us, event | category | flops | bytes accessed | tf_op | source)
XLA Modules:
  0.0 50.6 jit_solution(8575754468591558390)
XLA Ops:
  1.9 47.8 %shard_map.59 = (f32[64,1152]{1,0:T(8,128)S(1)}, f32[64,1152]{1,0:T(8,128)S(1)}) custom-call(bf16[64,1152]{1,0:T(8,128)(2,1)} %img_hbm.1, bf16[64,1152]{1,0:T(8,128)(2,1)} %txt_hbm.1, f32[1]{0:T(128)S(6)} %copy.6.temp_hbm, f32[1]{0:T(128)S(6)} %copy.7.bias_hbm), custom_call_target="tpu_custom_call" | custom-call | tf_op jit(solution)/shard_map/pallas_call | solution.py:411
  49.7 0.8 %shard_map.60 = (f32[64,1152]{1,0:T(8,128)}, f32[64,1152]{1,0:T(8,128)}) custom-call(f32[64,1152]{1,0:T(8,128)S(1)} %get-tuple-element.4.img_ref, f32[64,1152]{1,0:T(8,128)S(1)} %get-tuple-element.5.txt_ref), custom_call_target="tpu_custom_call" | custom-call | tf_op jit(solution)/shard_map/pallas_call | solution.py:434

commit v5 on v4

--- a/solution.py
+++ b/solution.py
@@ -288,14 +288,6 @@
     p_rows, q_rows, coef, p_part, q_part, p_send, q_send, p_back, q_back,
     pg_send, pg_recv, pr_send, pr_recv, qg_send, qg_recv, qr_send, qr_recv,
 ):
-    loads = [
-        pltpu.make_async_copy(here, there, in_sems.at[i])
-        for i, (here, there) in enumerate(
-            ((img_hbm, img_ref), (txt_hbm, txt_ref), (temp_hbm, temp_ref), (bias_hbm, bias_ref))
-        )
-    ]
-    for load in loads:
-        load.start()
     dp, mp = lax.axis_index("dp"), lax.axis_index("mp")
     core, z, x = dp % 2, (dp // 2) % NZ, (dp // (2 * NZ)) * 2 + mp // NY
     y = mp % NY
@@ -318,6 +310,14 @@
     for device in neighbours:
         pl.semaphore_signal(barrier, inc=1, device_id=device, device_id_type=MESH)
 
+    loads = [
+        pltpu.make_async_copy(here, there, in_sems.at[i])
+        for i, (here, there) in enumerate(
+            ((img_hbm, img_ref), (txt_hbm, txt_ref), (temp_hbm, temp_ref), (bias_hbm, bias_ref))
+        )
+    ]
+    for load in loads:
+        load.start()
     img = Side(IMG_UNITS, img_edges(), p_rows, p_part, p_send, p_back,
                (pg_send, pg_recv, pr_send, pr_recv), place)
     txt = Side(TXT_UNITS, txt_edges(), q_rows, q_part, q_send, q_back,

time: 50.7 us -> 50.7 us (level)
  no operation moved by 1% of the time
where the time goes in v5:
time: 50.7 us; the launch traced here: 50.6 us
  Pallas kernels  48.6 us (96%)
  between operations  1.93 us (4%)
    pallas_call x1, Pallas kernels, on_device(): pl.pallas_call(kernel, out_shape=[pltpu.VMEM((rows, width), jnp.float32)]...  47.8 us

profile of v5, /device:TPU:1, one launch (start us, length us, event | category | flops | bytes accessed | tf_op | source)
XLA Modules:
  0.0 50.6 jit_solution(12411253240115906248)
XLA Ops:
  1.9 47.8 %shard_map.59 = (f32[64,1152]{1,0:T(8,128)S(1)}, f32[64,1152]{1,0:T(8,128)S(1)}) custom-call(bf16[64,1152]{1,0:T(8,128)(2,1)} %img_hbm.1, bf16[64,1152]{1,0:T(8,128)(2,1)} %txt_hbm.1, f32[1]{0:T(128)S(6)} %copy.6.temp_hbm, f32[1]{0:T(128)S(6)} %copy.7.bias_hbm), custom_call_target="tpu_custom_call" | custom-call | tf_op jit(solution)/shard_map/pallas_call | solution.py:411
  49.7 0.8 %shard_map.60 = (f32[64,1152]{1,0:T(8,128)}, f32[64,1152]{1,0:T(8,128)}) custom-call(f32[64,1152]{1,0:T(8,128)S(1)} %get-tuple-element.4.img_ref, f32[64,1152]{1,0:T(8,128)S(1)} %get-tuple-element.5.txt_ref), custom_call_target="tpu_custom_call" | custom-call | tf_op jit(solution)/shard_map/pallas_call | solution.py:434

commit v6 on v5

--- a/solution.py
+++ b/solution.py
@@ -393,8 +393,9 @@
 
 def store_kernel(img_ref, txt_ref, img_out, txt_out, sems):
     stores = [
-        pltpu.make_async_copy(here, there, sems.at[i])
+        pltpu.make_async_copy(here.at[pl.ds(row, QUARTER)], there.at[pl.ds(row, QUARTER)], sems.at[i, row // QUARTER])
         for i, (here, there) in enumerate(((img_ref, img_out), (txt_ref, txt_out)))
+        for row in range(0, ROWS, QUARTER)
     ]
     for store in stores:
         store.start()
@@ -436,7 +437,7 @@
         out_shape=[jax.ShapeDtypeStruct((rows, width), jnp.float32)] * 2,
         in_specs=[vmem] * 2,
         out_specs=[anywhere] * 2,
-        scratch_shapes=[pltpu.SemaphoreType.DMA((2,))],
+        scratch_shapes=[pltpu.SemaphoreType.DMA((2, ROWS // QUARTER))],
     )(*(pltpu.with_memory_space_constraint(grad, pltpu.VMEM) for grad in grads))
 
 

time: 50.7 us -> 50.7 us (level)
  no operation moved by 1% of the time
where the time goes in v6:
time: 50.7 us; the launch traced here: 50.6 us
  Pallas kernels  48.7 us (96%)
  between operations  1.93 us (4%)
    pallas_call x1, Pallas kernels, on_device(): pl.pallas_call(kernel, out_shape=[pltpu.VMEM((rows, width), jnp.float32)]...  47.8 us

profile of v6, /device:TPU:1, one launch (start us, length us, event | category | flops | bytes accessed | tf_op | source)
XLA Modules:
  0.0 50.6 jit_solution(2471663055913681079)
XLA Ops:
  1.9 47.8 %shard_map.59 = (f32[64,1152]{1,0:T(8,128)S(1)}, f32[64,1152]{1,0:T(8,128)S(1)}) custom-call(bf16[64,1152]{1,0:T(8,128)(2,1)} %img_hbm.1, bf16[64,1152]{1,0:T(8,128)(2,1)} %txt_hbm.1, f32[1]{0:T(128)S(6)} %copy.6.temp_hbm, f32[1]{0:T(128)S(6)} %copy.7.bias_hbm), custom_call_target="tpu_custom_call" | custom-call | tf_op jit(solution)/shard_map/pallas_call | solution.py:412
  49.7 0.9 %shard_map.60 = (f32[64,1152]{1,0:T(8,128)}, f32[64,1152]{1,0:T(8,128)}) custom-call(f32[64,1152]{1,0:T(8,128)S(1)} %get-tuple-element.4.img_ref, f32[64,1152]{1,0:T(8,128)S(1)} %get-tuple-element.5.txt_ref), custom_call_target="tpu_custom_call" | custom-call | tf_op jit(solution)/shard_map/pallas_call | solution.py:435
